TPU v7x, 32 devices: a whole 2x2x4 slice. The times are simulated.
32 devices in a mesh: seq: 2 (over core), fsdp: 16 (over z, y, x).
Axes of the slice: x: 2, y: 2, z: 4, core: 2. Of those that a mesh axis runs over, the one named last changes fastest.
Arguments:
- tokens: bfloat16 [16, 1024, 1024], P('fsdp', 'seq'), may hold values from -6 to 6
- qkv_weight: bfloat16 [1024, 3072], P('fsdp'), may hold values from -0.1875 to 0.1875
- query_bias: bfloat16 [1024], P('fsdp'), may hold values from -1.5 to 1.5
- value_bias: bfloat16 [1024], P('fsdp'), may hold values from -1.5 to 1.5
- proj_weight: bfloat16 [1024, 1024], P('fsdp'), may hold values from -4 to 4
- proj_bias: bfloat16 [1024], P('fsdp'), may hold values from -1.5 to 1.5
- norm1_gain: bfloat16 [1024], P('fsdp'), may hold values from 0.25 to 1.75
- norm1_shift: bfloat16 [1024], P('fsdp'), may hold values from -1.5 to 1.5
- inner_weight: bfloat16 [1024, 4096], P('fsdp'), may hold values from -0.1875 to 0.1875
- inner_bias: bfloat16 [4096], P('fsdp'), may hold values from -2.5 to 2.5
- outer_weight: bfloat16 [4096, 1024], P('fsdp'), may hold values from -0.09375 to 0.09375
- outer_bias: bfloat16 [1024], P('fsdp'), may hold values from -1.5 to 1.5
- norm2_gain: bfloat16 [1024], P('fsdp'), may hold values from 0.25 to 1.75
- norm2_shift: bfloat16 [1024], P('fsdp'), may hold values from -1.5 to 1.5
- cotangent: bfloat16 [16, 1024, 1024], P('fsdp', 'seq'), may hold values from -6 to 6
Outputs:
- mixed: bfloat16 [16, 1024, 1024], P('fsdp', 'seq')
- input_grad: bfloat16 [16, 1024, 1024], P('fsdp', 'seq')
- qkv_grad: float32 [1024, 3072], P('fsdp')
- query_bias_grad: float32 [1024], P('fsdp')
- value_bias_grad: float32 [1024], P('fsdp')
- proj_grad: float32 [1024, 1024], P('fsdp')
- proj_bias_grad: float32 [1024], P('fsdp')
- norm1_gain_grad: float32 [1024], P('fsdp')
- norm1_shift_grad: float32 [1024], P('fsdp')
- inner_grad: float32 [1024, 4096], P('fsdp')
- inner_bias_grad: float32 [4096], P('fsdp')
- outer_grad: float32 [4096, 1024], P('fsdp')
- outer_bias_grad: float32 [1024], P('fsdp')
- norm2_gain_grad: float32 [1024], P('fsdp')
- norm2_shift_grad: float32 [1024], P('fsdp')
All inputs are finite; a program needn't handle non-finite values.
Results may differ from a plain program's by a relative error of at most 0.022.
Values may be sent and summed in bfloat16 or wider, within the bound.
A program may use at most 192 MiB of HBM per device.

v0:
```python
import jax
import jax.numpy as jnp
from jax import lax
from jax.sharding import PartitionSpec as P

HEAD_DIM = 64


EPSILON = 1e-12
LOWEST = -1e30


def layer_norm(values, gains, shifts):
    center = values - jnp.mean(values, axis=-1, keepdims=True)
    spread = jnp.mean(center * center, axis=-1, keepdims=True)
    return center * lax.rsqrt(spread + EPSILON) * gains + shifts


def gelu_exact(values):
    return jax.nn.gelu(values, approximate=False)


def by_blocks(step_fn, carried, pieces, block_rows):
    row_total = pieces[0].shape[1]
    number = row_total // block_rows
    stacked = tuple(
        (
            jnp.moveaxis(
                piece.reshape((piece.shape[0], number, block_rows) + piece.shape[2:]), 1, 0
            )
            for piece in pieces
        )
    )

    def advance(running, element):
        index_now, members = element
        return (step_fn(running, members, index_now * block_rows), None)

    carried, unused = lax.scan(advance, carried, (jnp.arange(number, dtype=jnp.int32), stacked))
    return carried


def on_device(
    tokens,
    qkv_weight,
    query_bias,
    value_bias,
    proj_weight,
    proj_bias,
    norm1_gain,
    norm1_shift,
    inner_weight,
    inner_bias,
    outer_weight,
    outer_bias,
    norm2_gain,
    norm2_shift,
    cotangent,
):
    seq_count = tokens.shape[0]
    token_rows = tokens.shape[1]
    feature_width = tokens.shape[2]
    all_rows = seq_count * token_rows
    head_count = feature_width // HEAD_DIM
    factor = HEAD_DIM ** (-0.5)
    inputs = tokens.reshape(all_rows, feature_width)
    (
        mix_all,
        query_shift,
        value_shift,
        proj_all,
        proj_shift,
        gain_one,
        shift_one,
        inner_all,
        inner_shift,
        outer_all,
        outer_shift,
        gain_two,
        shift_two,
    ) = (
        lax.all_gather(qkv_weight, "fsdp", axis=0, tiled=True),
        lax.all_gather(query_bias, "fsdp", axis=0, tiled=True),
        lax.all_gather(value_bias, "fsdp", axis=0, tiled=True),
        lax.all_gather(proj_weight, "fsdp", axis=0, tiled=True),
        lax.all_gather(proj_bias, "fsdp", axis=0, tiled=True),
        lax.all_gather(norm1_gain, "fsdp", axis=0, tiled=True),
        lax.all_gather(norm1_shift, "fsdp", axis=0, tiled=True),
        lax.all_gather(inner_weight, "fsdp", axis=0, tiled=True),
        lax.all_gather(inner_bias, "fsdp", axis=0, tiled=True),
        lax.all_gather(outer_weight, "fsdp", axis=0, tiled=True),
        lax.all_gather(outer_bias, "fsdp", axis=0, tiled=True),
        lax.all_gather(norm2_gain, "fsdp", axis=0, tiled=True),
        lax.all_gather(norm2_shift, "fsdp", axis=0, tiled=True),
    )
    gain_one = gain_one.astype(jnp.float32)
    shift_one = shift_one.astype(jnp.float32)
    gain_two = gain_two.astype(jnp.float32)
    shift_two = shift_two.astype(jnp.float32)
    joined = jnp.dot(inputs, mix_all, preferred_element_type=jnp.float32)
    queries = (joined[:, :feature_width] + query_shift).astype(jnp.bfloat16)
    key_rows = (
        joined[:, feature_width : 2 * feature_width]
        .astype(jnp.bfloat16)
        .reshape(seq_count, token_rows, feature_width)
    )
    value_rows = (
        (joined[:, 2 * feature_width :] + value_shift)
        .astype(jnp.bfloat16)
        .reshape(seq_count, token_rows, feature_width)
    )
    query_heads = queries.reshape(seq_count, token_rows, head_count, HEAD_DIM)
    start_state = (
        jnp.full((seq_count, head_count, token_rows), LOWEST, jnp.float32),
        jnp.zeros((seq_count, head_count, token_rows), jnp.float32),
        jnp.zeros((seq_count, head_count, token_rows, HEAD_DIM), jnp.float32),
    )

    def attend(carried, pieces, offset):
        maxima, totals, summed = carried
        remote_keys = pieces[0].reshape(seq_count, -1, head_count, HEAD_DIM)
        remote_values = pieces[1].reshape(seq_count, -1, head_count, HEAD_DIM)
        scores = (
            jnp.einsum(
                "sqhd,skhd->shqk", query_heads, remote_keys, preferred_element_type=jnp.float32
            )
            * factor
        )
        top_score = jnp.maximum(maxima, jnp.max(scores, axis=-1))
        fading = jnp.exp(maxima - top_score)
        raised = jnp.exp(scores - top_score[..., None])
        totals = totals * fading + jnp.sum(raised, axis=-1)
        summed = summed * fading[..., None] + jnp.einsum(
            "shqk,skhd->shqd",
            raised.astype(jnp.bfloat16),
            remote_values,
            preferred_element_type=jnp.float32,
        )
        return (top_score, totals, summed)

    maxima, totals, summed = by_blocks(
        attend,
        start_state,
        (
            lax.all_gather(key_rows, "seq", axis=1, tiled=True),
            lax.all_gather(value_rows, "seq", axis=1, tiled=True),
        ),
        token_rows,
    )
    log_total = maxima + jnp.log(totals)
    context_heads = (summed / totals[..., None]).transpose(0, 2, 1, 3)
    context = context_heads.reshape(all_rows, feature_width)
    context_low = context.astype(jnp.bfloat16)
    attended = jnp.dot(context_low, proj_all, preferred_element_type=jnp.float32) + proj_shift
    normed_one, first_pull = jax.vjp(
        layer_norm, inputs.astype(jnp.float32) + attended, gain_one, shift_one
    )
    normed_low = normed_one.astype(jnp.bfloat16)
    inner_pre = jnp.dot(normed_low, inner_all, preferred_element_type=jnp.float32) + inner_shift
    active, gelu_pull = jax.vjp(gelu_exact, inner_pre)
    active_low = active.astype(jnp.bfloat16)
    branch = jnp.dot(active_low, outer_all, preferred_element_type=jnp.float32) + outer_shift
    result, second_pull = jax.vjp(layer_norm, normed_one + branch, gain_two, shift_two)
    mix_all, proj_all, inner_all, outer_all = (
        lax.all_gather(qkv_weight, "fsdp", axis=0, tiled=True),
        lax.all_gather(proj_weight, "fsdp", axis=0, tiled=True),
        lax.all_gather(inner_weight, "fsdp", axis=0, tiled=True),
        lax.all_gather(outer_weight, "fsdp", axis=0, tiled=True),
    )
    upstream = cotangent.reshape(all_rows, feature_width).astype(jnp.float32)
    grad_two, grad_gain_two, grad_shift_two = second_pull(upstream)
    grad_two_low = grad_two.astype(jnp.bfloat16)
    grad_outer_shift = jnp.sum(grad_two_low.astype(jnp.float32), axis=0)
    grad_outer = jnp.dot(active_low.T, grad_two_low, preferred_element_type=jnp.float32)
    grad_active = jnp.dot(grad_two_low, outer_all.T, preferred_element_type=jnp.float32)
    (grad_inner_pre,) = gelu_pull(grad_active)
    inner_low = grad_inner_pre.astype(jnp.bfloat16)
    grad_inner_shift = jnp.sum(inner_low.astype(jnp.float32), axis=0)
    grad_inner = jnp.dot(normed_low.T, inner_low, preferred_element_type=jnp.float32)
    grad_first = grad_two + jnp.dot(inner_low, inner_all.T, preferred_element_type=jnp.float32)
    grad_one, grad_gain_one, grad_shift_one = first_pull(grad_first)
    grad_one_low = grad_one.astype(jnp.bfloat16)
    grad_proj_shift = jnp.sum(grad_one_low.astype(jnp.float32), axis=0)
    grad_proj = jnp.dot(context_low.T, grad_one_low, preferred_element_type=jnp.float32)
    grad_context = jnp.dot(grad_one_low, proj_all.T, preferred_element_type=jnp.float32).astype(
        jnp.bfloat16
    )
    grad_heads = grad_context.reshape(seq_count, token_rows, head_count, HEAD_DIM)
    row_delta = jnp.sum(grad_heads.astype(jnp.float32) * context_heads, axis=-1).transpose(0, 2, 1)
    length = token_rows * lax.axis_size("seq")
    back_state = (
        jnp.zeros((seq_count, head_count, token_rows, HEAD_DIM), jnp.float32),
        jnp.zeros((seq_count, length, 2 * feature_width), jnp.float32),
    )

    def attend_back(carried, pieces, offset):
        query_sum, pair_sum = carried
        remote_keys = pieces[0].reshape(seq_count, -1, head_count, HEAD_DIM)
        remote_values = pieces[1].reshape(seq_count, -1, head_count, HEAD_DIM)
        scores = (
            jnp.einsum(
                "sqhd,skhd->shqk", query_heads, remote_keys, preferred_element_type=jnp.float32
            )
            * factor
        )
        probabilities = jnp.exp(scores - log_total[..., None])
        prob_grad = jnp.einsum(
            "sqhd,skhd->shqk", grad_heads, remote_values, preferred_element_type=jnp.float32
        )
        score_grad = (probabilities * (prob_grad - row_delta[..., None])).astype(jnp.bfloat16)
        query_sum = (
            query_sum
            + jnp.einsum(
                "shqk,skhd->shqd", score_grad, remote_keys, preferred_element_type=jnp.float32
            )
            * factor
        )
        key_grad = (
            jnp.einsum(
                "shqk,sqhd->skhd", score_grad, query_heads, preferred_element_type=jnp.float32
            )
            * factor
        )
        value_grad = jnp.einsum(
            "shqk,sqhd->skhd",
            probabilities.astype(jnp.bfloat16),
            grad_heads,
            preferred_element_type=jnp.float32,
        )
        number = remote_keys.shape[1]
        update_rows = jnp.concatenate(
            [
                key_grad.reshape(seq_count, number, feature_width),
                value_grad.reshape(seq_count, number, feature_width),
            ],
            axis=2,
        )
        current = lax.dynamic_slice_in_dim(pair_sum, offset, number, 1)
        pair_sum = lax.dynamic_update_slice_in_dim(pair_sum, current + update_rows, offset, 1)
        return (query_sum, pair_sum)

    query_sum, pair_sum = by_blocks(
        attend_back,
        back_state,
        (
            lax.all_gather(key_rows, "seq", axis=1, tiled=True),
            lax.all_gather(value_rows, "seq", axis=1, tiled=True),
        ),
        token_rows,
    )
    own_pairs = (
        lax.psum_scatter(pair_sum.astype(jnp.bfloat16), "seq", scatter_dimension=1, tiled=True)
        .astype(jnp.float32)
        .reshape(all_rows, 2 * feature_width)
    )
    query_low = (
        query_sum.transpose(0, 2, 1, 3).reshape(all_rows, feature_width).astype(jnp.bfloat16)
    )
    key_low = own_pairs[:, :feature_width].astype(jnp.bfloat16)
    value_low = own_pairs[:, feature_width:].astype(jnp.bfloat16)
    joined_grad = jnp.concatenate([query_low, key_low, value_low], axis=1)
    grad_mix = jnp.dot(inputs.T, joined_grad, preferred_element_type=jnp.float32)
    grad_query_shift = jnp.sum(query_low.astype(jnp.float32), axis=0)
    grad_value_shift = jnp.sum(value_low.astype(jnp.float32), axis=0)
    input_grad = (
        grad_one + jnp.dot(joined_grad, mix_all.T, preferred_element_type=jnp.float32)
    ).astype(jnp.bfloat16)
    shares = (
        lax.psum_scatter(
            grad_mix.astype(jnp.bfloat16), "fsdp", scatter_dimension=0, tiled=True
        ).astype(jnp.float32),
        lax.psum_scatter(
            grad_query_shift.astype(jnp.bfloat16), "fsdp", scatter_dimension=0, tiled=True
        ).astype(jnp.float32),
        lax.psum_scatter(
            grad_value_shift.astype(jnp.bfloat16), "fsdp", scatter_dimension=0, tiled=True
        ).astype(jnp.float32),
        lax.psum_scatter(
            grad_proj.astype(jnp.bfloat16), "fsdp", scatter_dimension=0, tiled=True
        ).astype(jnp.float32),
        lax.psum_scatter(
            grad_proj_shift.astype(jnp.bfloat16), "fsdp", scatter_dimension=0, tiled=True
        ).astype(jnp.float32),
        lax.psum_scatter(
            grad_gain_one.astype(jnp.bfloat16), "fsdp", scatter_dimension=0, tiled=True
        ).astype(jnp.float32),
        lax.psum_scatter(
            grad_shift_one.astype(jnp.bfloat16), "fsdp", scatter_dimension=0, tiled=True
        ).astype(jnp.float32),
        lax.psum_scatter(
            grad_inner.astype(jnp.bfloat16), "fsdp", scatter_dimension=0, tiled=True
        ).astype(jnp.float32),
        lax.psum_scatter(
            grad_inner_shift.astype(jnp.bfloat16), "fsdp", scatter_dimension=0, tiled=True
        ).astype(jnp.float32),
        lax.psum_scatter(
            grad_outer.astype(jnp.bfloat16), "fsdp", scatter_dimension=0, tiled=True
        ).astype(jnp.float32),
        lax.psum_scatter(
            grad_outer_shift.astype(jnp.bfloat16), "fsdp", scatter_dimension=0, tiled=True
        ).astype(jnp.float32),
        lax.psum_scatter(
            grad_gain_two.astype(jnp.bfloat16), "fsdp", scatter_dimension=0, tiled=True
        ).astype(jnp.float32),
        lax.psum_scatter(
            grad_shift_two.astype(jnp.bfloat16), "fsdp", scatter_dimension=0, tiled=True
        ).astype(jnp.float32),
    )
    summed_up = (
        lax.psum(shares[0].astype(jnp.bfloat16), "seq").astype(jnp.float32),
        lax.psum(shares[1].astype(jnp.bfloat16), "seq").astype(jnp.float32),
        lax.psum(shares[2].astype(jnp.bfloat16), "seq").astype(jnp.float32),
        lax.psum(shares[3].astype(jnp.bfloat16), "seq").astype(jnp.float32),
        lax.psum(shares[4].astype(jnp.bfloat16), "seq").astype(jnp.float32),
        lax.psum(shares[5].astype(jnp.bfloat16), "seq").astype(jnp.float32),
        lax.psum(shares[6].astype(jnp.bfloat16), "seq").astype(jnp.float32),
        lax.psum(shares[7].astype(jnp.bfloat16), "seq").astype(jnp.float32),
        lax.psum(shares[8].astype(jnp.bfloat16), "seq").astype(jnp.float32),
        lax.psum(shares[9].astype(jnp.bfloat16), "seq").astype(jnp.float32),
        lax.psum(shares[10].astype(jnp.bfloat16), "seq").astype(jnp.float32),
        lax.psum(shares[11].astype(jnp.bfloat16), "seq").astype(jnp.float32),
        lax.psum(shares[12].astype(jnp.bfloat16), "seq").astype(jnp.float32),
    )
    return (
        result.astype(jnp.bfloat16).reshape(tokens.shape),
        input_grad.reshape(tokens.shape),
        summed_up[0],
        summed_up[1],
        summed_up[2],
        summed_up[3],
        summed_up[4],
        summed_up[5],
        summed_up[6],
        summed_up[7],
        summed_up[8],
        summed_up[9],
        summed_up[10],
        summed_up[11],
        summed_up[12],
    )


def solution(mesh):
    in_specs = (
        P("fsdp", "seq", None),
        P("fsdp", None),
        P("fsdp"),
        P("fsdp"),
        P("fsdp", None),
        P("fsdp"),
        P("fsdp"),
        P("fsdp"),
        P("fsdp", None),
        P("fsdp"),
        P("fsdp", None),
        P("fsdp"),
        P("fsdp"),
        P("fsdp"),
        P("fsdp", "seq", None),
    )
    out_specs = (
        P("fsdp", "seq", None),
        P("fsdp", "seq", None),
        P("fsdp", None),
        P("fsdp"),
        P("fsdp"),
        P("fsdp", None),
        P("fsdp"),
        P("fsdp"),
        P("fsdp"),
        P("fsdp", None),
        P("fsdp"),
        P("fsdp", None),
        P("fsdp"),
        P("fsdp"),
        P("fsdp"),
    )
    return jax.shard_map(
        on_device, mesh=mesh, in_specs=in_specs, out_specs=out_specs, check_vma=False
    )
```

profile of v0, /device:TPU:0, one launch (start us, length us, event | category | flops | bytes accessed | tf_op | source)
XLA Modules:
  0.0 1308.0 jit_solution(15326165827265557573)
XLA Ops:
  15.8 80.1 %all-reduce.18 = (bf16[1024]{0:T(1024)(128)(2,1)S(1)}, bf16[1024]{0:T(1024)(128)(2,1)S(1)}, bf16[1024]{0:T(1024)(128)(2,1)S(1)}, bf16[1024]{0:T(1024)(128)(2,1)S...) all-reduce(bf16[1024]{0:T(1024)(128)(2,1)S(1)} %dynamic-update-slic, ...), channel_id=1, replica_groups=mesh['seq'=2,'fsdp'=16] {'fsdp'}, use_global_device_ids=true, to_apply=%add | all-reduce | flops 7168 | bytes 28672
  96.0 12.6 all-gather.10.cloned.1.call-done
  123.4 38.3 %all-gather.2 = bf16[16,1,256]{2,1,0:T(2,128)(2,1)S(1)} all-gather(bf16[1,1,256]{2,1,0:T(2,128)(2,1)S(1)} %reshape.273), channel_id=1, replica_groups=mesh['seq'=2,'fsdp'=16] {'fsdp'}, dimensions={0}, use_global_device_ids=true | all-gather | bytes 8704 | tf_op jit(solution)/shard_map/all_gather | solution.py:90
  171.3 58.3 %while.28 = (s32[]{:T(128)}, f32[1,16,512]{2,1,0:T(8,128)S(1)}, f32[1,16,512]{2,1,0:T(8,128)S(1)}, f32[1,16,512,64]{2,3,1,0:T(8,128)}, bf16[2,1,512,1024]{2,3,1,...) while((s32[]{:T(128)}, f32[1,16,512]{2,1,0:T(8,128)S(1)}, ...), condition=%wide.region_3.4_spmd.clone, body=%wide.region_0.3_spmd.clone.sunk | while | flops 1108918272 | bytes 62390376 | solution.py:39
  173.0 8.1 bitcast_reduce_fusion.2
  181.1 10.2 bitcast_add_fusion.7
  191.3 8.6 fusion.109
  201.7 8.1 bitcast_reduce_fusion.2
  209.8 11.0 bitcast_add_fusion.7
  220.9 8.6 fusion.109
  237.4 83.2 %all-gather.14.cloned.1.call-done = bf16[1024,4096]{1,0:T(8,128)(2,1)} async-done(((bf16[64,4096]{1,0:T(8,128)(2,1)}), bf16[1024,4096]{1,0:T(8,128)(2,1)}) %all-gather.14.cloned.1.call-update) | async-done | bytes 8388624 | tf_op jit(solution)/shard_map/all_gather | solution.py:89
  320.6 27.6 %multiply_convert_fusion.1 = (bf16[512,4096]{1,0:T(8,128)(2,1)}, f32[512,4096]{1,0:T(8,128)}, f32[512,4096]{1,0:T(8,128)}) fusion(f32[4096]{0:T(1024)S(1)} %bitcast.210, bf16[1024,4096]{1,0:T(8,128)(2,1)} %all-gather.14.cloned.1.call-done, f32[512,1024]{1,0:T(8,128)S(1)} %get-tuple-element.361, f32[1024]{0:T(1024)S(1)} %convert_element_type.221, ...), kind=kOutput, calls=%fused_computation.41 | convolution fusion | flops 4436000768 | bytes 31485952 | tf_op jit(solution)/shard_map/dot_general | solution.py:159
  348.2 86.0 %all-gather.16.cloned.1.call-done = bf16[4096,1024]{1,0:T(8,128)(2,1)} async-done(((bf16[256,1024]{1,0:T(8,128)(2,1)}), bf16[4096,1024]{1,0:T(8,128)(2,1)}) %all-gather.16.cloned.1.call-update) | async-done | bytes 8388624 | tf_op jit(solution)/shard_map/all_gather | solution.py:91
  434.3 8.5 fusion.61
  446.3 14.4 %fusion.53 = (bf16[4096]{0:T(1024)(128)(2,1)}, bf16[512,4096]{1,0:T(8,128)(2,1)S(1)}) fusion(f32[512,4096]{1,0:T(8,128)} %get-tuple-element.349, f32[512,4096]{1,0:T(8,128)} %get-tuple-element.362, f32[4096]{0:T(1024)S(1)} %bitcast.211, bf16[512,1024]{1,0:T(8,128)(2,1)S(1)} %get-tuple-element.337, bf16[4096,1024]{1,0:T(8,128)(2,1)} %all-gather.16.cloned.1.call-done), kind=kOutput, calls=%fused_computation.113 | convolution fusion | flops 4328517632 | bytes 30433280 | tf_op jit(solution)/shard_map/dot_general | solution.py:175
  460.7 9.7 multiply_reduce_fusion
  481.9 90.7 %while.29 = (s32[]{:T(128)}, f32[1,16,512,64]{2,3,1,0:T(8,128)}, f32[1,1024,2048]{1,2,0:T(8,128)}, bf16[2,1,512,1024]{2,3,1,0:T(8,128)(2,1)}, bf16[1,512,16,64]{...) while((s32[]{:T(128)}, f32[1,16,512,64]{2,3,1,0:T(8,128)}, ...), condition=%wide.region_14.15_spmd.clone, body=%wide.region_13.14_spmd.clone.sunk | while | flops 2722103296 | bytes 191988064 | solution.py:39
  489.1 9.2 multiply_convert_fusion.3
  507.1 7.7 fusion.121
  534.1 9.2 multiply_convert_fusion.3
  552.0 7.7 fusion.121
  580.4 8.6 reduce-scatter.8.cloned.1.call-done
  589.0 7.9 convert_bitcast_fusion
  596.9 8.6 copy.57
  610.7 9.2 convolution_convert_fusion.1
  621.1 9.0 convolution_convert_fusion
  630.3 122.3 %reduce-scatter.16.cloned.1.call-done = bf16[64,3072]{1,0:T(8,128)(2,1)} async-done(((bf16[1024,3072]{1,0:T(8,128)(2,1)}), bf16[64,3072]{1,0:T(8,128)(2,1)}) %reduce-scatter.16.cloned.1.call-update) | async-done | bytes 393232
  754.8 79.9 %reduce-scatter.10.cloned.1.call-done = bf16[64,1024]{1,0:T(8,128)(2,1)} async-done(((bf16[1024,1024]{1,0:T(8,128)(2,1)}), bf16[64,1024]{1,0:T(8,128)(2,1)}) %reduce-scatter.10.cloned.1.call-update) | async-done | bytes 131088 | tf_op jit(solution)/shard_map/reduce_scatter | solution.py:278
  834.7 177.3 %reduce-scatter.12.cloned.1.call-done = bf16[64,4096]{1,0:T(8,128)(2,1)} async-done(((bf16[1024,4096]{1,0:T(8,128)(2,1)}), bf16[64,4096]{1,0:T(8,128)(2,1)}) %reduce-scatter.12.cloned.1.call-update) | async-done | bytes 524304 | tf_op jit(solution)/shard_map/reduce_scatter | solution.py:290
  1012.0 182.7 %reduce-scatter.14.cloned.1.call-done = bf16[256,1024]{1,0:T(8,128)(2,1)} async-done(((bf16[4096,1024]{1,0:T(8,128)(2,1)}), bf16[256,1024]{1,0:T(8,128)(2,1)}) %reduce-scatter.14.cloned.1.call-update) | async-done | bytes 524304 | tf_op jit(solution)/shard_map/reduce_scatter | solution.py:296
  1198.1 77.5 %all-reduce.17 = (bf16[1024]{0:T(1024)(128)(2,1)S(1)}, bf16[1024]{0:T(1024)(128)(2,1)S(1)}, bf16[1024]{0:T(1024)(128)(2,1)S(1)}, bf16[1024]{0:T(1024)(128)(2,1)S...) all-reduce(bf16[1024]{0:T(1024)(128)(2,1)S(1)} %dynamic-update-slic, ...), channel_id=1, replica_groups=mesh['seq'=2,'fsdp'=16] {'fsdp'}, use_global_device_ids=true, to_apply=%add.7 | all-reduce | flops 13312 | bytes 53248
  1285.1 8.5 fusion.40
  (245 shorter events, 148.7 us)
Async XLA Ops:
  7.2 101.4 %all-gather.10.cloned.1.call-start = ((), (), s32[]{:S(2)}) async-start(), calls=%async_computation.5 | async-start | bytes 6684672 | tf_op jit(solution)/shard_map/all_gather | solution.py:82
  7.9 155.5 %all-gather.20.cloned.1.call-start = ((), (), s32[]{:S(2)}) async-start(), calls=%async_computation.14 | async-start | bytes 3145728 | tf_op jit(solution)/shard_map/all_gather | solution.py:146
  118.6 48.7 %all-gather.18.cloned.1.call-start = ((), (), s32[]{:S(2)}) async-start(), calls=%async_computation.13 | async-start | bytes 3145728 | tf_op jit(solution)/shard_map/all_gather | solution.py:145
  121.4 111.0 %all-gather.12.cloned.1.call-start = ((), (), s32[]{:S(2)}) async-start(), calls=%async_computation.6 | async-start | bytes 2228224 | tf_op jit(solution)/shard_map/all_gather | solution.py:85
  122.0 198.6 %all-gather.14.cloned.1.call-start = ((), (), s32[]{:S(2)}) async-start(), calls=%async_computation.7 | async-start | bytes 8912896 | tf_op jit(solution)/shard_map/all_gather | solution.py:89
  122.6 311.6 %all-gather.16.cloned.1.call-start = ((), (), s32[]{:S(2)}) async-start(), calls=%async_computation.8 | async-start | bytes 8912896 | tf_op jit(solution)/shard_map/all_gather | solution.py:91
  123.2 465.8 %reduce-scatter.8.cloned.1.call-start = ((), (), s32[]{:S(2)}) async-start(), calls=%async_computation.9 | async-start | bytes 6291456 | tf_op jit(solution)/shard_map/reduce_scatter | solution.py:252
  123.3 347.1 %copy-start.30 = (f32[1024]{0:T(1024)}, f32[1024]{0:T(1024)S(1)}, u32[]{:S(2)}) copy-start(f32[1024]{0:T(1024)S(1)} %convert_element_type.220) | copy-start | bytes 12292
  123.3 310.9 %copy-start.40 = (f32[1024]{0:T(1024)}, f32[1024]{0:T(1024)S(1)}, u32[]{:S(2)}) copy-start(f32[1024]{0:T(1024)S(1)} %convert_element_type.221) | copy-start | bytes 12292
  236.0 234.4 %copy-start.8 = (f32[512,1024]{1,0:T(8,128)}, f32[512,1024]{1,0:T(8,128)S(1)}, u32[]{:S(2)}) copy-start(f32[512,1024]{1,0:T(8,128)S(1)} %get-tuple-element.361) | copy-start | bytes 6291460
  236.0 234.4 %copy-start.28 = (f32[512]{0:T(512)}, f32[512]{0:T(512)S(1)}, u32[]{:S(2)}) copy-start(f32[512]{0:T(512)S(1)} %broadcast_multiply_fusion.1) | copy-start | bytes 6148
  236.3 234.0 %copy-start.34 = (f32[512]{0:T(512)}, f32[512]{0:T(512)S(1)}, u32[]{:S(2)}) copy-start(f32[512]{0:T(512)S(1)} %fusion.45) | copy-start | bytes 6148
  320.6 113.7 %copy-start.42 = (f32[1024]{0:T(1024)S(1)}, f32[1024]{0:T(1024)}, u32[]{:S(2)}) copy-start(f32[1024]{0:T(1024)} %convert_element_type.225) | copy-start | bytes 12292
  578.6 174.0 %reduce-scatter.16.cloned.1.call-start = ((), (), s32[]{:S(2)}) async-start(), calls=%async_computation.15 | async-start | bytes 6684672
  605.6 229.1 %reduce-scatter.10.cloned.1.call-start = ((), (), s32[]{:S(2)}) async-start(), calls=%async_computation.10 | async-start | bytes 2228224 | tf_op jit(solution)/shard_map/reduce_scatter | solution.py:278
  610.6 401.4 %reduce-scatter.12.cloned.1.call-start = ((), (), s32[]{:S(2)}) async-start(), calls=%async_computation.11 | async-start | bytes 8912896 | tf_op jit(solution)/shard_map/reduce_scatter | solution.py:290
  619.9 574.7 %reduce-scatter.14.cloned.1.call-start = ((), (), s32[]{:S(2)}) async-start(), calls=%async_computation.12 | async-start | bytes 8912896 | tf_op jit(solution)/shard_map/reduce_scatter | solution.py:296
  630.1 564.6 %copy-start.11 = (bf16[1,512,1024]{2,1,0:T(8,128)(2,1)S(1)}, bf16[1,512,1024]{2,1,0:T(8,128)(2,1)}, u32[]{:S(2)}) copy-start(bf16[1,512,1024]{2,1,0:T(8,128)(2,1)} %param.33) | copy-start | bytes 3145732
  630.1 566.1 %copy-start.46 = (bf16[64]{0:T(256)(128)(2,1)S(1)}, bf16[64]{0:T(256)(128)(2,1)}, u32[]{:S(2)}) copy-start(bf16[64]{0:T(256)(128)(2,1)} %param.32) | copy-start | bytes 388
  630.2 567.9 %copy-start.36 = (bf16[1024]{0:T(1024)(128)(2,1)S(1)}, bf16[1024]{0:T(1024)(128)(2,1)}, u32[]{:S(2)}) copy-start(bf16[1024]{0:T(1024)(128)(2,1)} %get-tuple-element.267) | copy-start | bytes 6148
  630.2 567.9 %copy-start.37 = (bf16[1024]{0:T(1024)(128)(2,1)S(1)}, bf16[1024]{0:T(1024)(128)(2,1)}, u32[]{:S(2)}) copy-start(bf16[1024]{0:T(1024)(128)(2,1)} %get-tuple-element.336) | copy-start | bytes 6148
  630.2 567.9 %copy-start.38 = (bf16[1024]{0:T(1024)(128)(2,1)S(1)}, bf16[1024]{0:T(1024)(128)(2,1)}, u32[]{:S(2)}) copy-start(bf16[1024]{0:T(1024)(128)(2,1)} %get-tuple-element.340) | copy-start | bytes 6148
  630.2 567.9 %copy-start.39 = (bf16[4096]{0:T(1024)(128)(2,1)S(1)}, bf16[4096]{0:T(1024)(128)(2,1)}, u32[]{:S(2)}) copy-start(bf16[4096]{0:T(1024)(128)(2,1)} %get-tuple-element.338) | copy-start | bytes 24580
  630.2 567.9 %copy-start.43 = (bf16[1024]{0:T(1024)(128)(2,1)S(1)}, bf16[1024]{0:T(1024)(128)(2,1)}, u32[]{:S(2)}) copy-start(bf16[1024]{0:T(1024)(128)(2,1)} %get-tuple-element.265) | copy-start | bytes 6148
  630.2 567.9 %copy-start.44 = (bf16[1024]{0:T(1024)(128)(2,1)S(1)}, bf16[1024]{0:T(1024)(128)(2,1)}, u32[]{:S(2)}) copy-start(bf16[1024]{0:T(1024)(128)(2,1)} %get-tuple-element.269) | copy-start | bytes 6148
  630.2 653.5 %copy-start.7 = (f32[512,1024]{1,0:T(8,128)S(1)}, f32[512,1024]{1,0:T(8,128)}, u32[]{:S(2)}) copy-start(f32[512,1024]{1,0:T(8,128)} %copy-done.6) | copy-start | bytes 6291460
  630.2 653.5 %copy-start.23 = (f32[1024]{0:T(1024)S(1)}, f32[1024]{0:T(1024)}, u32[]{:S(2)}) copy-start(f32[1024]{0:T(1024)} %convert_element_type.226) | copy-start | bytes 12292
  630.2 653.5 %copy-start.25 = (f32[512]{0:T(512)S(1)}, f32[512]{0:T(512)}, u32[]{:S(2)}) copy-start(f32[512]{0:T(512)} %copy-done.24) | copy-start | bytes 6148
  630.3 653.4 %copy-start.27 = (f32[512]{0:T(512)S(1)}, f32[512]{0:T(512)}, u32[]{:S(2)}) copy-start(f32[512]{0:T(512)} %copy-done.26) | copy-start | bytes 6148
  630.3 654.8 %copy-start.33 = (f32[512]{0:T(512)S(1)}, f32[512]{0:T(512)}, u32[]{:S(2)}) copy-start(f32[512]{0:T(512)} %copy-done.32) | copy-start | bytes 6148
  630.3 663.3 %all-reduce.23.cloned.1.call-start = ((), (), s32[]{:S(2)}) async-start(), calls=%async_computation.16 | async-start | bytes 3932160 | tf_op jit(solution)/shard_map/psum | solution.py:310
  1194.9 90.2 %copy-start.17 = (bf16[1,16,512,64]{2,3,1,0:T(8,128)(2,1)S(1)}, bf16[1,16,512,64]{2,3,1,0:T(8,128)(2,1)}, u32[]{:S(2)}) copy-start(bf16[1,16,512,64]{2,3,1,0:T(8,128)(2,1)} %copy-done.16) | copy-start | bytes 3145732
  (33 other events, 173.8 us)
Sparse Core Ops, SparseCore 0:
  10.8 97.7 all-gather.9
  118.8 9.1 all-gather.19
  130.1 11.7 all-gather.17
  144.5 61.8 all-gather.11
  209.1 111.4 all-gather.13
  323.2 111.0 all-gather.15
  578.7 10.2 reduce-scatter.7
  605.7 146.8 reduce-scatter.15
  755.0 79.6 reduce-scatter.9
  836.9 174.9 reduce-scatter.11
  1014.4 180.2 reduce-scatter.13
  1197.8 23.5 all-reduce.22
where the time goes:
time: 1310 us
  waiting for transfers between devices  755 us (58%)
  matrix products  216 us (16%)
  blocking collectives  199 us (15%)
  other arithmetic  62.8 us (5%)
  local copies, waits for them, and re-layouts  55.9 us (4%)
  between operations  17.2 us (1%)
    reduce_scatter x1, waiting for transfers between devices, on_device(): lax.psum_scatter(grad_outer.astype(jnp.bfloat16), 'fsdp', scatter_dimensi...  183 us
    reduce_scatter x1, waiting for transfers between devices, on_device(): lax.psum_scatter(grad_inner.astype(jnp.bfloat16), 'fsdp', scatter_dimensi...  177 us
    unnamed x2, blocking collectives  158 us
    unnamed x13, waiting for transfers between devices  125 us
    all_gather x1, waiting for transfers between devices, on_device(): lax.all_gather(outer_weight, 'fsdp', axis=0, tiled=True)  86 us
    all_gather x1, waiting for transfers between devices, on_device(): lax.all_gather(inner_weight, 'fsdp', axis=0, tiled=True)  83.2 us
    reduce_scatter x1, waiting for transfers between devices, on_device(): lax.psum_scatter(grad_proj.astype(jnp.bfloat16), 'fsdp', scatter_dimensio...  79.9 us
    all_gather x1, blocking collectives, on_device(): lax.all_gather(inner_bias, 'fsdp', axis=0, tiled=True)  38.3 us
  transfers between devices with their start and end apart: 12, of which 8 were waited for; matrix products, arithmetic and copies ran while one was open for 12% of the time, Pallas kernels for 0%

commit v1 on v0

v1 whole, which is shorter than its diff:
```python
import jax
import jax.numpy as jnp
from jax import lax
from jax.experimental import pallas as pl
from jax.experimental.pallas import tpu as pltpu
from jax.sharding import PartitionSpec as P

HEAD_DIM = 64
EPSILON = 1e-12
F32 = jnp.float32
LOW = jnp.bfloat16


def layer_norm(values, gains, shifts):
    center = values - jnp.mean(values, axis=-1, keepdims=True)
    spread = jnp.mean(center * center, axis=-1, keepdims=True)
    return center * lax.rsqrt(spread + EPSILON) * gains + shifts


def gelu_exact(values):
    return jax.nn.gelu(values, approximate=False)


def fsdp_swap(array, bits):
    count, span = lax.axis_size("seq"), lax.axis_size("fsdp")
    pairs = [
        (s * span + f, s * span + (f ^ bits[s & 1])) for s in range(count) for f in range(span)
    ]
    return lax.ppermute(array, ("seq", "fsdp"), pairs)


def seq_swap(array, bits):
    count = lax.axis_size("seq")
    return lax.ppermute(array, "seq", [(s, s ^ bits) for s in range(count)])


def high_bits():
    bit, bits = lax.axis_size("fsdp") // 2, []
    while bit > 2:
        bits.append(bit)
        bit //= 2
    return bits


def places():
    own = lax.axis_index("fsdp")
    even = lax.axis_index("seq") % 2 == 0
    along_x, along_y = own % 2, own // 2 % 2
    return own, even, along_x, along_y


def gather_seq(part):
    mine, bit = lax.axis_index("seq"), 1
    while bit < lax.axis_size("seq"):
        other = seq_swap(part, bit)
        first = mine // bit % 2 == 0
        part = jnp.concatenate(
            [jnp.where(first, part, other), jnp.where(first, other, part)], axis=1
        )
        bit *= 2
    return part


def gather_weight(shard):
    own, even, along_x, along_y = places()
    width = shard.shape[1] // lax.axis_size("seq")
    held = lax.dynamic_slice_in_dim(shard, lax.axis_index("seq") * width, width, 1)[None]
    rows = shard.shape[0]
    for bit in high_bits():
        other = fsdp_swap(held, (bit, bit))
        first = own // bit % 2 == 0
        held = jnp.stack(
            [jnp.where(first, held, other), jnp.where(first, other, held)], axis=1
        ).reshape(-1, rows, width)
    other = fsdp_swap(held, (1, 2))
    first = jnp.where(even, along_x, along_y) == 0
    held = jnp.stack([jnp.where(first, held, other), jnp.where(first, other, held)], axis=1)
    other = fsdp_swap(held, (2, 1))
    first = jnp.where(even, along_y, along_x) == 0
    near, far = jnp.where(first, held, other), jnp.where(first, other, held)
    whole = jnp.stack(
        [
            near[:, 0],
            jnp.where(even, near[:, 1], far[:, 0]),
            jnp.where(even, far[:, 0], near[:, 1]),
            far[:, 1],
        ],
        axis=1,
    )
    return gather_seq(whole.reshape(-1, width))


def add_swapped(keep, send, bits):
    return keep.astype(F32) + fsdp_swap(send.astype(LOW), bits).astype(F32)


def pick(array, index, axis):
    return lax.dynamic_index_in_dim(array, index, axis, keepdims=False)


def scatter_product(left, right):
    own, even, along_x, along_y = places()
    mine, bit = lax.axis_index("seq"), lax.axis_size("seq") // 2
    half = right.shape[1] // 2
    upper = mine // bit % 2

    def product(start):
        columns = lax.dynamic_slice_in_dim(right, start, half, 1)
        return lax.dot_general(
            left, columns, (((0,), (0,)), ((), ())), preferred_element_type=F32
        )

    arrived = seq_swap(product((1 - upper) * half).astype(LOW), bit)
    total = product(upper * half) + arrived.astype(F32)
    while bit > 1:
        bit //= 2
        half //= 2
        upper = mine // bit % 2
        keep = lax.dynamic_slice_in_dim(total, upper * half, half, 1)
        send = lax.dynamic_slice_in_dim(total, (1 - upper) * half, half, 1)
        total = keep + seq_swap(send.astype(LOW), bit).astype(F32)
    span = lax.axis_size("fsdp")
    rows = total.shape[0] // span
    total = total.astype(LOW).reshape(span // 4, 4, rows, half)
    keep = [jnp.where(even, along_y * 2 + k, k * 2 + along_x) for k in (0, 1)]
    send = [jnp.where(even, (1 - along_y) * 2 + k, k * 2 + 1 - along_x) for k in (0, 1)]
    total = add_swapped(
        jnp.stack([pick(total, place, 1) for place in keep], axis=1),
        jnp.stack([pick(total, place, 1) for place in send], axis=1),
        (2, 1),
    ).astype(LOW)
    here = jnp.where(even, along_x, along_y)
    total = add_swapped(pick(total, here, 1), pick(total, 1 - here, 1), (1, 2))
    for bit in reversed(high_bits()):
        total = total.astype(LOW).reshape(-1, 2, rows, half)
        here = own // bit % 2
        total = add_swapped(pick(total, here, 1), pick(total, 1 - here, 1), (bit, bit))
    return gather_seq(total.reshape(rows, half).astype(LOW)).astype(F32)


def gather_vectors(vectors):
    own = lax.axis_index("fsdp")
    held = jnp.concatenate(vectors)[None]
    bit = lax.axis_size("fsdp") // 2
    while bit >= 1:
        other = fsdp_swap(held, (bit, bit))
        first = own // bit % 2 == 0
        held = jnp.stack(
            [jnp.where(first, held, other), jnp.where(first, other, held)], axis=1
        ).reshape(-1, held.shape[1])
        bit //= 2
    whole, start = [], 0
    for vector in vectors:
        size = vector.shape[0]
        whole.append(held[:, start : start + size].reshape(-1))
        start += size
    return whole


def scatter_vectors(vectors):
    own, span = lax.axis_index("fsdp"), lax.axis_size("fsdp")
    total = jnp.concatenate([vector.reshape(span, -1) for vector in vectors], axis=1)
    bit = 1
    while bit < lax.axis_size("seq"):
        total = total + seq_swap(total, bit)
        bit *= 2
    bit = span // 2
    while bit >= 1:
        total = total.reshape(2, -1, total.shape[-1])
        here = own // bit % 2
        total = pick(total, here, 0) + fsdp_swap(pick(total, 1 - here, 0), (bit, bit))
        bit //= 2
    total, shares, start = total.reshape(-1), [], 0
    for vector in vectors:
        size = vector.shape[0] // span
        shares.append(total[start : start + size])
        start += size
    return shares


def product_of(left, right, left_dim, right_dim):
    return lax.dot_general(
        left, right, (((left_dim,), (right_dim,)), ((), ())), preferred_element_type=F32
    )


def attend_kernel(query_ref, key_ref, value_ref, context_ref, log_ref):
    factor = HEAD_DIM ** (-0.5)
    for head in range(128 // HEAD_DIM):
        lanes = slice(head * HEAD_DIM, (head + 1) * HEAD_DIM)
        scores = product_of(query_ref[:, lanes], key_ref[:, lanes], 1, 1) * factor
        top = jnp.max(scores, axis=1, keepdims=True)
        raised = jnp.exp(scores - top)
        total = jnp.sum(raised, axis=1, keepdims=True)
        summed = product_of(raised.astype(LOW), value_ref[:, lanes], 1, 0)
        context_ref[:, lanes] = summed / total
        log_ref[:, lanes] = jnp.broadcast_to(top + jnp.log(total), summed.shape)


def attend_back_kernel(
    query_ref, key_ref, value_ref, grad_ref, context_ref, log_ref, dq_ref, dk_ref, dv_ref
):
    factor = HEAD_DIM ** (-0.5)
    for head in range(128 // HEAD_DIM):
        lanes = slice(head * HEAD_DIM, (head + 1) * HEAD_DIM)
        queries, keys, values = query_ref[:, lanes], key_ref[:, lanes], value_ref[:, lanes]
        grads = grad_ref[:, lanes]
        delta = jnp.sum(grads.astype(F32) * context_ref[:, lanes], axis=1, keepdims=True)
        log_total = log_ref[:, head * HEAD_DIM : head * HEAD_DIM + 1]
        probs = jnp.exp(product_of(queries, keys, 1, 1) * factor - log_total)
        prob_grad = product_of(grads, values, 1, 1)
        score_grad = (probs * (prob_grad - delta)).astype(LOW)
        dv_ref[:, lanes] = product_of(probs.astype(LOW), grads, 0, 0).astype(LOW)
        dq_ref[:, lanes] = (product_of(score_grad, keys, 1, 0) * factor).astype(LOW)
        dk_ref[:, lanes] = (product_of(score_grad, queries, 0, 0) * factor).astype(LOW)


def attention_call(kernel, dots, row_inputs, pair_rows, out_shape):
    seqs, rows, width = row_inputs[0].shape
    length = pair_rows.shape[1]
    steps = width // 128

    def block(size, shift):
        return pl.BlockSpec((None, size, 128), lambda s, h: (s, 0, h + shift))

    in_specs = [block(rows, 0), block(length, 0), block(length, steps)]
    in_specs += [block(rows, 0)] * (len(row_inputs) - 1)
    return pl.pallas_call(
        kernel,
        grid=(seqs, steps),
        in_specs=in_specs,
        out_specs=[block(shape.shape[1], 0) for shape in out_shape],
        out_shape=out_shape,
        compiler_params=pltpu.CompilerParams(vmem_limit_bytes=40 * 1024 * 1024),
        cost_estimate=pl.CostEstimate(
            flops=8 * dots * seqs * rows * length * width,
            bytes_accessed=4 * seqs * (rows + length) * width * 2,
            transcendentals=seqs * rows * length * width // HEAD_DIM,
        ),
    )(row_inputs[0], pair_rows, pair_rows, *row_inputs[1:])


def on_device(
    tokens,
    qkv_weight,
    query_bias,
    value_bias,
    proj_weight,
    proj_bias,
    norm1_gain,
    norm1_shift,
    inner_weight,
    inner_bias,
    outer_weight,
    outer_bias,
    norm2_gain,
    norm2_shift,
    cotangent,
):
    seq_count, token_rows, width = tokens.shape
    all_rows = seq_count * token_rows
    members = lax.axis_size("seq")
    inputs = tokens.reshape(all_rows, width)
    mix_all = gather_weight(qkv_weight)
    (
        query_shift,
        value_shift,
        proj_shift,
        gain_one,
        shift_one,
        inner_shift,
        outer_shift,
        gain_two,
        shift_two,
    ) = gather_vectors(
        [
            query_bias,
            value_bias,
            proj_bias,
            norm1_gain,
            norm1_shift,
            inner_bias,
            outer_bias,
            norm2_gain,
            norm2_shift,
        ]
    )
    proj_all = gather_weight(proj_weight)
    inner_all = gather_weight(inner_weight)
    outer_all = gather_weight(outer_weight)
    gain_one, shift_one = gain_one.astype(F32), shift_one.astype(F32)
    gain_two, shift_two = gain_two.astype(F32), shift_two.astype(F32)
    joined_shift = jnp.concatenate([query_shift, jnp.zeros_like(query_shift), value_shift])
    joined = (jnp.dot(inputs, mix_all, preferred_element_type=F32) + joined_shift).astype(LOW)
    queries = joined[:, :width].reshape(seq_count, token_rows, width)
    own_pairs = joined[:, width:].reshape(seq_count, token_rows, 2 * width)
    pairs = jnp.concatenate(
        [own_pairs] + [seq_swap(own_pairs, j) for j in range(1, members)], axis=1
    )
    length = token_rows * members
    rows_f32 = jax.ShapeDtypeStruct((seq_count, token_rows, width), F32)
    context, log_total = attention_call(attend_kernel, 2, [queries], pairs, [rows_f32, rows_f32])
    context_low = context.astype(LOW).reshape(all_rows, width)
    attended = jnp.dot(context_low, proj_all, preferred_element_type=F32) + proj_shift
    normed_one, first_pull = jax.vjp(
        layer_norm, inputs.astype(F32) + attended, gain_one, shift_one
    )
    normed_low = normed_one.astype(LOW)
    inner_pre = jnp.dot(normed_low, inner_all, preferred_element_type=F32) + inner_shift
    active, gelu_pull = jax.vjp(gelu_exact, inner_pre)
    active_low = active.astype(LOW)
    branch = jnp.dot(active_low, outer_all, preferred_element_type=F32) + outer_shift
    result, second_pull = jax.vjp(layer_norm, normed_one + branch, gain_two, shift_two)
    upstream = cotangent.reshape(all_rows, width).astype(F32)
    grad_two, grad_gain_two, grad_shift_two = second_pull(upstream)
    grad_two_low = grad_two.astype(LOW)
    grad_outer_shift = jnp.sum(grad_two_low.astype(F32), axis=0)
    grad_outer = scatter_product(active_low, grad_two_low)
    grad_active = lax.dot_general(
        grad_two_low, outer_all, (((1,), (1,)), ((), ())), preferred_element_type=F32
    )
    (grad_inner_pre,) = gelu_pull(grad_active)
    inner_low = grad_inner_pre.astype(LOW)
    grad_inner_shift = jnp.sum(inner_low.astype(F32), axis=0)
    grad_inner = scatter_product(normed_low, inner_low)
    grad_first = grad_two + jnp.dot(inner_low, inner_all.T, preferred_element_type=F32)
    grad_one, grad_gain_one, grad_shift_one = first_pull(grad_first)
    grad_one_low = grad_one.astype(LOW)
    grad_proj_shift = jnp.sum(grad_one_low.astype(F32), axis=0)
    grad_proj = scatter_product(context_low, grad_one_low)
    grad_context = jnp.dot(grad_one_low, proj_all.T, preferred_element_type=F32).astype(LOW)
    pair_out = jax.ShapeDtypeStruct((seq_count, length, width), LOW)
    query_low, key_sums, value_sums = attention_call(
        attend_back_kernel,
        5,
        [queries, grad_context.reshape(seq_count, token_rows, width), context, log_total],
        pairs,
        [jax.ShapeDtypeStruct((seq_count, token_rows, width), LOW), pair_out, pair_out],
    )
    query_low = query_low.reshape(all_rows, width)

    def to_owner(sums):
        total = sums[:, :token_rows].astype(F32)
        for j in range(1, members):
            block = sums[:, j * token_rows : (j + 1) * token_rows]
            total = total + seq_swap(block, j).astype(F32)
        return total.astype(LOW).reshape(all_rows, width)

    key_low, value_low = to_owner(key_sums), to_owner(value_sums)
    joined_grad = jnp.concatenate([query_low, key_low, value_low], axis=1)
    grad_mix = scatter_product(inputs, joined_grad)
    grad_query_shift = jnp.sum(query_low.astype(F32), axis=0)
    grad_value_shift = jnp.sum(value_low.astype(F32), axis=0)
    input_grad = (
        grad_one + jnp.dot(joined_grad, mix_all.T, preferred_element_type=F32)
    ).astype(LOW)
    (
        grad_query_shift,
        grad_value_shift,
        grad_proj_shift,
        grad_gain_one,
        grad_shift_one,
        grad_inner_shift,
        grad_outer_shift,
        grad_gain_two,
        grad_shift_two,
    ) = scatter_vectors(
        [
            grad_query_shift,
            grad_value_shift,
            grad_proj_shift,
            grad_gain_one,
            grad_shift_one,
            grad_inner_shift,
            grad_outer_shift,
            grad_gain_two,
            grad_shift_two,
        ]
    )
    return (
        result.astype(LOW).reshape(tokens.shape),
        input_grad.reshape(tokens.shape),
        grad_mix,
        grad_query_shift,
        grad_value_shift,
        grad_proj,
        grad_proj_shift,
        grad_gain_one,
        grad_shift_one,
        grad_inner,
        grad_inner_shift,
        grad_outer,
        grad_outer_shift,
        grad_gain_two,
        grad_shift_two,
    )


def solution(mesh):
    in_specs = (
        P("fsdp", "seq", None),
        P("fsdp", None),
        P("fsdp"),
        P("fsdp"),
        P("fsdp", None),
        P("fsdp"),
        P("fsdp"),
        P("fsdp"),
        P("fsdp", None),
        P("fsdp"),
        P("fsdp", None),
        P("fsdp"),
        P("fsdp"),
        P("fsdp"),
        P("fsdp", "seq", None),
    )
    out_specs = (
        P("fsdp", "seq", None),
        P("fsdp", "seq", None),
        P("fsdp", None),
        P("fsdp"),
        P("fsdp"),
        P("fsdp", None),
        P("fsdp"),
        P("fsdp"),
        P("fsdp"),
        P("fsdp", None),
        P("fsdp"),
        P("fsdp", None),
        P("fsdp"),
        P("fsdp"),
        P("fsdp"),
    )
    return jax.shard_map(
        on_device, mesh=mesh, in_specs=in_specs, out_specs=out_specs, check_vma=False
    )
```

time: 1310 us -> 523 us (0.40)
  waiting for transfers between devices: 755 us -> 219 us
  blocking collectives: 199 us -> 0 us
  matrix products: 216 us -> 104 us
  starting transfers between devices: 0.7 us -> 63.2 us
  Pallas kernels: 0 us -> 51.6 us
  local copies, waits for them, and re-layouts: 55.9 us -> 31.9 us
  other arithmetic: 62.8 us -> 45.2 us
  between operations: 17.2 us -> 2.59 us
    reduce_scatter x4 -> x0, waiting for transfers between devices: 448 us -> none  [the longest x1 183 us: on_device(): lax.psum_scatter(grad_outer.astype(jnp.bfloat16), 'fsdp', scatter_dimensi...]
    ppermute x0 -> x56, waiting for transfers between devices: none -> 219 us  [the longest x40 216 us: fsdp_swap(): return lax.ppermute(array, ('seq', 'fsdp'), pairs)]
    all_gather x6 -> x0, waiting for transfers between devices: 182 us -> none  [the longest x1 86 us: on_device(): lax.all_gather(outer_weight, 'fsdp', axis=0, tiled=True)]
    unnamed x2 -> x0, blocking collectives: 158 us -> none
    unnamed x13 -> x0, waiting for transfers between devices: 125 us -> none
    dot_general x26 -> x16, matrix products: 216 us -> 104 us  [the longest x8 32.3 us: product(): lax.dot_general(left, columns, (((0,), (0,)), ((), ())), preferred_elemen...]
    ppermute x0 -> x56, starting transfers between devices: none -> 63.2 us  [the longest x40 52.2 us: fsdp_swap(): return lax.ppermute(array, ('seq', 'fsdp'), pairs)]
    pallas_call x0 -> x2, Pallas kernels: none -> 51.6 us  [attention_call(): pl.pallas_call(kernel, grid=(seqs, steps), in_specs=in_specs, out_specs=[...]
  transfers between devices with their start and end apart: 12 -> 56, of which waited for: 8 -> 25; matrix products, arithmetic and copies ran while one was open for 12% -> 19% of each run, Pallas kernels for 0% -> 0%
where the time goes in v1:
time: 523 us; the launch traced here: 517 us
  waiting for transfers between devices  219 us (42%)
  matrix products  104 us (20%)
  starting transfers between devices  63.2 us (12%)
  Pallas kernels  51.6 us (10%)
  other arithmetic  45.2 us (9%)
  local copies, waits for them, and re-layouts  31.9 us (6%)
    ppermute x40, waiting for transfers between devices, fsdp_swap(): return lax.ppermute(array, ('seq', 'fsdp'), pairs)  216 us
    ppermute x40, starting transfers between devices, fsdp_swap(): return lax.ppermute(array, ('seq', 'fsdp'), pairs)  52.2 us
    pallas_call x2, Pallas kernels, attention_call(): pl.pallas_call(kernel, grid=(seqs, steps), in_specs=in_specs, out_specs=[...  51.6 us
    dot_general x8, matrix products, product(): lax.dot_general(left, columns, (((0,), (0,)), ((), ())), preferred_elemen...  32.3 us
    dot_general x1, matrix products, on_device(): jnp.dot(normed_low, inner_all, preferred_element_type=F32) + inner_shift  27.8 us
    select_n x8, other arithmetic, gather_seq(): jnp.where(first, part, other)  17.9 us
    dot_general x1, matrix products, on_device(): lax.dot_general(grad_two_low, outer_all, (((1,), (1,)), ((), ())), prefer...  13.5 us
    ppermute x16, starting transfers between devices, seq_swap(): return lax.ppermute(array, 'seq', [(s, s ^ bits) for s in range(count)])  11 us
  transfers between devices with their start and end apart: 56, of which 25 were waited for; matrix products, arithmetic and copies ran while one was open for 19% of the time, Pallas kernels for 0%

profile of v1, /device:TPU:0, one launch (start us, length us, event | category | flops | bytes accessed | tf_op | source)
XLA Modules:
  0.0 517.4 jit_solution(4943122083000409077)
XLA Ops:
  0.7 6.1 %concatenate.48 = bf16[768]{0:T(1024)(128)(2,1)S(1)} concatenate(bf16[64]{0:T(256)(128)(2,1)} %param.17, bf16[64]{0:T(256)(128)(2,1)} %param.18, bf16[64]{0:T(256)(128)(2,1)} %param.20, bf16[64]{0:T(256)(128)(2,1)} %param.21, bf16[64]{0:T(256)(128)(2,1)} %param.22, bf16[256]{0:T(256)(128)(2,1)} %param.24, bf16[64]{0:T(256)(128)(2,1)} %param.26, bf16[64]{0:T(256)(128)(2,1)} %param.27, ...), dimensions={0} | concatenate | bytes 3072 | tf_op jit(solution)/shard_map/concatenate | solution.py:143
  6.8 4.1 collective-permute-start.5
  23.2 4.6 collective-permute-start.20
  31.8 8.3 %collective-permute-done.10 = bf16[1,64,512]{2,1,0:T(8,128)(2,1)S(1)} collective-permute-done((bf16[1,64,512]{2,1,0:T(8,128)(2,1)S(1)}, bf16[1,64,512]{2,1,0:T(8,128)(2,1)S(1)}, u32[]{:S(2)}, u32[]{:S(2)}) %collective-permute-start.10) | collective-permute-done | bytes 65568 | tf_op jit(solution)/shard_map/ppermute | solution.py:29
  40.3 11.3 %collective-permute-done.11 = bf16[2,64,512]{2,1,0:T(8,128)(2,1)S(1)} collective-permute-done((bf16[2,64,512]{2,1,0:T(8,128)(2,1)S(1)}, bf16[2,64,512]{2,1,0:T(8,128)(2,1)S(1)}, u32[]{:S(2)}, u32[]{:S(2)}) %collective-permute-start.11) | collective-permute-done | bytes 131104 | tf_op jit(solution)/shard_map/ppermute | solution.py:29
  59.7 5.6 %collective-permute-done.1 = bf16[2,64,1536]{2,1,0:T(8,128)(2,1)S(1)} collective-permute-done((bf16[2,64,1536]{2,1,0:T(8,128)(2,1)S(1)}, bf16[2,64,1536]{2,1,0:T(8,128)(2,1)S(1)}, u32[]{:S(2)}, u32[]{:S(2)}) %collective-permute-start.1) | collective-permute-done | bytes 393248 | tf_op jit(solution)/shard_map/ppermute | solution.py:29
  66.1 10.5 %collective-permute-done.16 = bf16[2,64,2048]{2,1,0:T(8,128)(2,1)S(1)} collective-permute-done((bf16[2,64,2048]{2,1,0:T(8,128)(2,1)S(1)}, bf16[2,64,2048]{2,1,0:T(8,128)(2,1)S(1)}, u32[]{:S(2)}, u32[]{:S(2)}) %collective-permute-start.16) | collective-permute-done | bytes 524320 | tf_op jit(solution)/shard_map/ppermute | solution.py:29
  77.3 9.3 %collective-permute-done.21 = bf16[2,256,512]{2,1,0:T(8,128)(2,1)S(1)} collective-permute-done((bf16[2,256,512]{2,1,0:T(8,128)(2,1)S(1)}, bf16[2,256,512]{2,1,0:T(8,128)(2,1)S(1)}, u32[]{:S(2)}, u32[]{:S(2)}) %collective-permute-start.21) | collective-permute-done | bytes 524320 | tf_op jit(solution)/shard_map/ppermute | solution.py:29
  89.4 4.3 collective-permute-done.17
  96.7 19.4 %collective-permute-done.22 = bf16[4,256,512]{2,1,0:T(8,128)(2,1)S(1)} collective-permute-done((bf16[4,256,512]{2,1,0:T(8,128)(2,1)S(1)}, bf16[4,256,512]{2,1,0:T(8,128)(2,1)S(1)}, u32[]{:S(2)}, u32[]{:S(2)}) %collective-permute-start.22) | collective-permute-done | bytes 1048608 | tf_op jit(solution)/shard_map/ppermute | solution.py:29
  121.3 17.6 %collective-permute-done.18 = bf16[4,2,64,2048]{3,2,0,1:T(8,128)(2,1)S(1)} collective-permute-done((bf16[4,2,64,2048]{3,2,0,1:T(8,128)(2,1)S(1)}, bf16[4,2,64,2048]{3,2,0,1:T(8,128)(2,1)S(1)}, u32[]{:S(2)}, u32[]{:S(2)}) %collective-permute-start.18) | collective-permute-done | bytes 2097184 | tf_op jit(solution)/shard_map/ppermute | solution.py:29
  145.9 15.5 %collective-permute-done.23 = bf16[4,2,256,512]{3,2,0,1:T(8,128)(2,1)S(1)} collective-permute-done((bf16[4,2,256,512]{3,2,0,1:T(8,128)(2,1)S(1)}, bf16[4,2,256,512]{3,2,0,1:T(8,128)(2,1)S(1)}, u32[]{:S(2)}, u32[]{:S(2)}) %collective-permute-start.23) | collective-permute-done | bytes 2097184 | tf_op jit(solution)/shard_map/ppermute | solution.py:29
  183.8 8.6 %broadcast_select_fusion.1 = (bf16[4096,512]{1,0:T(8,128)(2,1)}, bf16[4096,512]{1,0:T(8,128)(2,1)}) fusion(bf16[4096,512]{1,0:T(8,128)(2,1)} %collective-permute-done.24, pred[]{:T(512)S(6)} %eq.111, bf16[4,4,256,512]{3,2,1,0:T(8,128)(2,1)} %copy.69), kind=kLoop, calls=%fused_computation.37 | loop fusion | flops 4194304 | bytes 16777216 | tf_op jit(solution)/shard_map/jit(_where)/select_n | solution.py:58
  193.0 20.2 %shard_map.262 = (f32[1,512,1024]{2,1,0:T(8,128)S(1)}, f32[1,512,1024]{2,1,0:T(8,128)S(1)}) custom-call(bf16[1,512,1024]{2,1,0:T(8,128)(2,1)S(1)} %slice_bitcast_fusion.1.query_ref, bf16[1,1024,2048]{2,1,0:T(8,128)(2,1)S(1)} %pad_maximum_fusion.7.key_ref.value_ref, bf16[1,1024,2048]{2,1,0:T(8,128)(2,1)S(1)} %pad_maximum_fusion.7.key_ref.value_ref), custom_call_target="tpu_custom_call" | custom-call | flops 8589934592 | bytes 12582912 | tf_op jit(solution)/shard_map/pallas_call | solution.py:228
  215.0 27.8 %multiply_convert_fusion = (bf16[512,4096]{1,0:T(8,128)(2,1)}, f32[512,4096]{1,0:T(8,128)}, f32[512,4096]{1,0:T(8,128)}) fusion(f32[4096]{0:T(1024)S(1)} %bitcast.352, bf16[1024,2048]{1,0:T(8,128)(2,1)S(1)} %get-tuple-element.45, bf16[1024,2048]{1,0:T(8,128)(2,1)S(1)} %get-tuple-element.44, f32[512,1024]{1,0:T(8,128)S(1)} %get-tuple-element.148, ...), kind=kOutput, calls=%fused_computation.8 | convolution fusion | flops 4452777984 | bytes 31485952 | tf_op jit(solution)/shard_map/dot_general | solution.py:309
  242.9 6.9 %fusion.98 = (f32[512]{0:T(512)S(1)}, f32[512,1024]{1,0:T(8,128)S(1)}) fusion(f32[1024]{0:T(1024)S(1)} %reshape.430, bf16[512,4096]{1,0:T(8,128)(2,1)} %get-tuple-element.40, bf16[4096,512]{1,0:T(8,128)(2,1)S(1)} %copy-done.16, bf16[4096,512]{1,0:T(8,128)(2,1)S(1)} %copy-done.15, f32[1024]{0:T(1024)S(1)} %reshape.428, f32[1024]{0:T(1024)S(1)} %reshape.427, ...), kind=kOutput, calls=%fused_computation.315 | convolution fusion | flops 4315414016 | bytes 16795648 | tf_op jit(solution)/shard_map/dot_general | solution.py:312
  253.2 13.5 %convert_reduce_fusion = (f32[4096]{0:T(1024)S(1)}, bf16[512,4096]{1,0:T(8,128)(2,1)}) fusion(f32[512,4096]{1,0:T(8,128)} %get-tuple-element.41, bf16[512,1024]{1,0:T(8,128)(2,1)S(1)} %get-tuple-element.31, bf16[4096,512]{1,0:T(8,128)(2,1)} %get-tuple-element.43, bf16[4096,512]{1,0:T(8,128)(2,1)} %get-tuple-element.42, f32[512,4096]{1,0:T(8,128)} %get-tuple-element.149, ...), kind=kOutput, calls=%fused_computation.6 | convolution fusion | flops 4347392000 | bytes 30441472 | tf_op jit(solution)/shard_map/dot_general | solution.py:319
  266.8 9.2 %multiply_reduce_fusion = (f32[1024]{0:T(1024)S(1)}, f32[512]{0:T(512)S(1)}, f32[1024]{0:T(1024)S(1)}, f32[512,1024]{1,0:T(8,128)S(1)}) fusion(f32[512,1024]{1,0:T(8,128)S(1)} %copy-done.9, f32[512]{0:T(512)S(1)} %fusion.80, f32[512]{0:T(512)S(1)} %broadcast_multiply_fusion.1, f32[1024]{0:T(1024)S(1)} %reshape.427, ...), kind=kOutput, calls=%fused_computation.75 | convolution fusion | flops 4316984832 | bytes 18894848 | tf_op jit(solution)/shard_map/dot_general | solution.py:326
  280.3 31.4 %shard_map.263 = (bf16[1,512,1024]{2,1,0:T(8,128)(2,1)S(1)}, bf16[1,1024,1024]{2,1,0:T(8,128)(2,1)S(1)}, bf16[1,1024,1024]{2,1,0:T(8,128)(2,1)S(1)}) custom-call(bf16[1,512,1024]{2,1,0:T(8,128)(2,1)S(1)} %slice_bitcast_fusion.1.query_ref, bf16[1,1024,2048]{2,1,0:T(8,128)(2,1)} %copy-done, bf16[1,1024,2048]{2,1,0:T(8,128)(2,1)} %copy-done, ...), custom_call_target="tpu_custom_call" | custom-call | flops 21474836480 | bytes 12582912 | tf_op jit(solution)/shard_map/pallas_call | solution.py:228
  317.2 6.9 %convolution_convert_fusion.1 = bf16[1024,2048]{1,0:T(8,128)(2,1)} fusion(bf16[512,4096]{1,0:T(8,128)(2,1)} %get-tuple-element.154, s32[]{:T(128)S(6)} %select_n.861, f32[512,1024]{1,0:T(8,128)} %copy-done.8, f32[1024]{0:T(1024)S(1)} %reshape.428, f32[1024]{0:T(1024)S(1)} %reshape.427, f32[512]{0:T(512)S(1)} %fusion.80, f32[512]{0:T(512)S(1)} %broadcast_multiply_fusion.1), kind=kOutput, calls=%fused_computation.42 | convolution fusion | flops 2152202240 | bytes 8400900 | tf_op jit(solution)/shard_map/dot_general | solution.py:109
  324.7 4.5 convolution_convert_fusion
  349.4 7.9 %fusion.32 = bf16[1,512,1024]{2,1,0:T(8,128)(2,1)} fusion(bf16[1024,1536]{1,0:T(8,128)(2,1)} %copy-done.23, bf16[1024,1536]{1,0:T(8,128)(2,1)} %copy-done.22, f32[512,1024]{1,0:T(8,128)S(1)} %copy-done.12, f32[512]{0:T(512)S(1)} %negate_multiply_fusion.1, bf16[512,1024]{1,0:T(8,128)(2,1)} %copy-done.19, bf16[512,1024]{1,0:T(8,128)(2,1)} %copy-done.18, ...), kind=kOutput, calls=%fused_computation.108 | convolution fusion | flops 3244818432 | bytes 12584960 | tf_op jit(solution)/shard_map/dot_general | solution.py:355
  362.4 4.2 collective-permute-done.40
  384.6 4.8 add_convert_fusion.1
  390.9 11.6 %collective-permute-done.28 = bf16[4,2,64,1536]{3,2,0,1:T(8,128)(2,1)S(1)} collective-permute-done((bf16[4,2,64,1536]{3,2,0,1:T(8,128)(2,1)S(1)}, bf16[4,2,64,1536]{3,2,0,1:T(8,128)(2,1)S(1)}, u32[]{:S(2)}, u32[]{:S(2)}) %collective-permute-start.28) | collective-permute-done | bytes 1572896 | tf_op jit(solution)/shard_map/ppermute | solution.py:29
  405.0 4.7 add_convert_fusion
  411.2 12.6 %collective-permute-done.29 = bf16[4,64,1536]{2,1,0:T(8,128)(2,1)S(1)} collective-permute-done((bf16[4,64,1536]{2,1,0:T(8,128)(2,1)S(1)}, bf16[4,64,1536]{2,1,0:T(8,128)(2,1)S(1)}, u32[]{:S(2)}, u32[]{:S(2)}) %collective-permute-start.29) | collective-permute-done | bytes 786464 | tf_op jit(solution)/shard_map/ppermute | solution.py:29
  426.6 6.8 %collective-permute-done.45 = bf16[4,2,64,2048]{3,2,0,1:T(8,128)(2,1)S(1)} collective-permute-done((bf16[4,2,64,2048]{3,2,0,1:T(8,128)(2,1)S(1)}, bf16[4,2,64,2048]{3,2,0,1:T(8,128)(2,1)S(1)}, u32[]{:S(2)}, u32[]{:S(2)}) %collective-permute-start.45) | collective-permute-done | bytes 2097184 | tf_op jit(solution)/shard_map/ppermute | solution.py:29
  436.8 30.3 %collective-permute-done.51 = bf16[4,2,256,512]{3,2,0,1:T(8,128)(2,1)S(1)} collective-permute-done((bf16[4,2,256,512]{3,2,0,1:T(8,128)(2,1)S(1)}, bf16[4,2,256,512]{3,2,0,1:T(8,128)(2,1)S(1)}, u32[]{:S(2)}, u32[]{:S(2)}) %collective-permute-start.51) | collective-permute-done | bytes 2097184 | tf_op jit(solution)/shard_map/ppermute | solution.py:29
  471.5 11.1 %collective-permute-done.52 = bf16[4,256,512]{2,1,0:T(8,128)(2,1)S(1)} collective-permute-done((bf16[4,256,512]{2,1,0:T(8,128)(2,1)S(1)}, bf16[4,256,512]{2,1,0:T(8,128)(2,1)S(1)}, u32[]{:S(2)}, u32[]{:S(2)}) %collective-permute-start.52) | collective-permute-done | bytes 1048608 | tf_op jit(solution)/shard_map/ppermute | solution.py:29
  486.5 15.5 %collective-permute-done.53 = bf16[2,256,512]{2,1,0:T(8,128)(2,1)S(1)} collective-permute-done((bf16[2,256,512]{2,1,0:T(8,128)(2,1)S(1)}, bf16[2,256,512]{2,1,0:T(8,128)(2,1)S(1)}, u32[]{:S(2)}, u32[]{:S(2)}) %collective-permute-start.53) | collective-permute-done | bytes 524320 | tf_op jit(solution)/shard_map/ppermute | solution.py:29
  503.4 10.8 %collective-permute-done.54 = bf16[1,256,512]{2,1,0:T(8,128)(2,1)S(1)} collective-permute-done((bf16[1,256,512]{2,1,0:T(8,128)(2,1)S(1)}, bf16[1,256,512]{2,1,0:T(8,128)(2,1)S(1)}, u32[]{:S(2)}, u32[]{:S(2)}) %collective-permute-start.54) | collective-permute-done | bytes 262176 | tf_op jit(solution)/shard_map/ppermute | solution.py:29
  (349 shorter events, 148.8 us)
Async XLA Ops:
  11.9 41.5 %collective-permute-start.15 = (bf16[1,64,2048]{2,1,0:T(8,128)(2,1)S(1)}, bf16[1,64,2048]{2,1,0:T(8,128)(2,1)S(1)}, u32[]{:S(2)}, u32[]{:S(2)}) collective-permute-start(bf16[1,64,2048]{2,1,0:T(8,128)(2,1)S(1)} %dynamic-slice_bitcast_fusion.24), channel_id=1, source_target_pairs={{0,8},{1,9},{2,10},{3,11},{4,12},{5,13},{6,14},{7,15},{8,0},{9,1},... | collective-permute-start | bytes 786440 | tf_op jit(solution)/shard_map/ppermute | solution.py:29
  12.9 27.2 %collective-permute-start.10 = (bf16[1,64,512]{2,1,0:T(8,128)(2,1)S(1)}, bf16[1,64,512]{2,1,0:T(8,128)(2,1)S(1)}, u32[]{:S(2)}, u32[]{:S(2)}) collective-permute-start(bf16[1,64,512]{2,1,0:T(8,128)(2,1)S(1)} %dynamic-slice_bitcast_fusion.27), channel_id=1, source_target_pairs={{0,8},{1,9},{2,10},{3,11},{4,12},{5,13},{6,14},{7,15},{8,0},{9,1},... | collective-permute-start | bytes 196616 | tf_op jit(solution)/shard_map/ppermute | solution.py:29
  18.4 34.8 %collective-permute-start = (bf16[1,64,1536]{2,1,0:T(8,128)(2,1)S(1)}, bf16[1,64,1536]{2,1,0:T(8,128)(2,1)S(1)}, u32[]{:S(2)}, u32[]{:S(2)}) collective-permute-start(bf16[1,64,1536]{2,1,0:T(8,128)(2,1)S(1)} %dynamic-slice_bitcast_fusion.25), channel_id=1, source_target_pairs={{0,8},{1,9},{2,10},{3,11},{4,12},{5,13},{6,14},{7,15},{8,0},{9,1},... | collective-permute-start | bytes 589832 | tf_op jit(solution)/shard_map/ppermute | solution.py:29
  23.2 32.4 %collective-permute-start.20 = (bf16[1,256,512]{2,1,0:T(8,128)(2,1)S(1)}, bf16[1,256,512]{2,1,0:T(8,128)(2,1)S(1)}, u32[]{:S(2)}, u32[]{:S(2)}) collective-permute-start(bf16[1,256,512]{2,1,0:T(8,128)(2,1)S(1)} %dynamic-slice_bitcast_fusion.23), channel_id=1, source_target_pairs={{0,8},{1,9},{2,10},{3,11},{4,12},{5,13},{6,14},{7,15},{8,0},{9,1},... | collective-permute-start | bytes 786440 | tf_op jit(solution)/shard_map/ppermute | solution.py:29
  53.6 23.0 %collective-permute-start.16 = (bf16[2,64,2048]{2,1,0:T(8,128)(2,1)S(1)}, bf16[2,64,2048]{2,1,0:T(8,128)(2,1)S(1)}, u32[]{:S(2)}, u32[]{:S(2)}) collective-permute-start(bf16[2,64,2048]{2,1,0:T(8,128)(2,1)S(1)} %maximum_bitcast_fusion), channel_id=1, source_target_pairs={{0,4},{1,5},{2,6},{3,7},{4,0},{5,1},{6,2},{7,3},{8,12},{9,13},{10,... | collective-permute-start | bytes 1572872 | tf_op jit(solution)/shard_map/ppermute | solution.py:29
  55.8 30.8 %collective-permute-start.21 = (bf16[2,256,512]{2,1,0:T(8,128)(2,1)S(1)}, bf16[2,256,512]{2,1,0:T(8,128)(2,1)S(1)}, u32[]{:S(2)}, u32[]{:S(2)}) collective-permute-start(bf16[2,256,512]{2,1,0:T(8,128)(2,1)S(1)} %maximum_bitcast_fusion.1), channel_id=1, source_target_pairs={{0,4},{1,5},{2,6},{3,7},{4,0},{5,1},{6,2},{7,3},{8,12},{9,13},{10,... | collective-permute-start | bytes 1572872 | tf_op jit(solution)/shard_map/ppermute | solution.py:29
  58.1 30.2 %collective-permute-start.13 = (bf16[4,2,64,512]{3,2,0,1:T(8,128)(2,1)S(1)}, bf16[4,2,64,512]{3,2,0,1:T(8,128)(2,1)S(1)}, u32[]{:S(2)}, u32[]{:S(2)}) collective-permute-start(bf16[4,2,64,512]{3,2,0,1:T(8,128)(2,1)S(1)} %pad_maximum_fusion.37), channel_id=1, source_target_pairs={{0,2},{1,3},{2,0},{3,1},{4,6},{5,7},{6,4},{7,5},{8,10},{9,11},{10,... | collective-permute-start | bytes 1572872 | tf_op jit(solution)/shard_map/ppermute | solution.py:29
  65.5 22.9 %collective-permute-start.2 = (bf16[4,64,1536]{2,1,0:T(8,128)(2,1)S(1)}, bf16[4,64,1536]{2,1,0:T(8,128)(2,1)S(1)}, u32[]{:S(2)}, u32[]{:S(2)}) collective-permute-start(bf16[4,64,1536]{2,1,0:T(8,128)(2,1)S(1)} %bitcast.348), channel_id=1, source_target_pairs={{0,1},{1,0},{2,3},{3,2},{4,5},{5,4},{6,7},{7,6},{8,9},{9,8},{10,11... | collective-permute-start | bytes 2359304 | tf_op jit(solution)/shard_map/ppermute | solution.py:29
  76.8 16.9 %collective-permute-start.17 = (bf16[4,64,2048]{2,1,0:T(8,128)(2,1)S(1)}, bf16[4,64,2048]{2,1,0:T(8,128)(2,1)S(1)}, u32[]{:S(2)}, u32[]{:S(2)}) collective-permute-start(bf16[4,64,2048]{2,1,0:T(8,128)(2,1)S(1)} %bitcast.340), channel_id=1, source_target_pairs={{0,1},{1,0},{2,3},{3,2},{4,5},{5,4},{6,7},{7,6},{8,9},{9,8},{10,11... | collective-permute-start | bytes 3145736 | tf_op jit(solution)/shard_map/ppermute | solution.py:29
  86.8 29.3 %collective-permute-start.22 = (bf16[4,256,512]{2,1,0:T(8,128)(2,1)S(1)}, bf16[4,256,512]{2,1,0:T(8,128)(2,1)S(1)}, u32[]{:S(2)}, u32[]{:S(2)}) collective-permute-start(bf16[4,256,512]{2,1,0:T(8,128)(2,1)S(1)} %bitcast.339), channel_id=1, source_target_pairs={{0,1},{1,0},{2,3},{3,2},{4,5},{5,4},{6,7},{7,6},{8,9},{9,8},{10,11... | collective-permute-start | bytes 3145736 | tf_op jit(solution)/shard_map/ppermute | solution.py:29
  88.8 29.2 %collective-permute-start.3 = (bf16[4,2,64,1536]{3,2,0,1:T(8,128)(2,1)S(1)}, bf16[4,2,64,1536]{3,2,0,1:T(8,128)(2,1)S(1)}, u32[]{:S(2)}, u32[]{:S(2)}) collective-permute-start(bf16[4,2,64,1536]{3,2,0,1:T(8,128)(2,1)S(1)} %pad_maximum_fusion.21), channel_id=1, source_target_pairs={{0,2},{1,3},{2,0},{3,1},{4,6},{5,7},{6,4},{7,5},{8,10},{9,11},{10,... | collective-permute-start | bytes 4718600 | tf_op jit(solution)/shard_map/ppermute | solution.py:29
  94.1 44.8 %collective-permute-start.18 = (bf16[4,2,64,2048]{3,2,0,1:T(8,128)(2,1)S(1)}, bf16[4,2,64,2048]{3,2,0,1:T(8,128)(2,1)S(1)}, u32[]{:S(2)}, u32[]{:S(2)}) collective-permute-start(bf16[4,2,64,2048]{3,2,0,1:T(8,128)(2,1)S(1)} %pad_maximum_fusion.17), channel_id=1, source_target_pairs={{0,2},{1,3},{2,0},{3,1},{4,6},{5,7},{6,4},{7,5},{8,10},{9,11},{10,... | collective-permute-start | bytes 6291464 | tf_op jit(solution)/shard_map/ppermute | solution.py:29
  96.7 72.0 %collective-permute-start.14 = (bf16[1024,512]{1,0:T(8,128)(2,1)}, bf16[1024,512]{1,0:T(8,128)(2,1)}, u32[]{:S(2)}, u32[]{:S(2)}) collective-permute-start(bf16[1024,512]{1,0:T(8,128)(2,1)} %bitcast.35), channel_id=1, source_target_pairs={{0,16},{16,0},{1,17},{17,1},{2,18},{18,2},{3,19},{19,3},{4,20},{20... | collective-permute-start | bytes 3145736 | tf_op jit(solution)/shard_map/ppermute | solution.py:34
  116.5 44.8 %collective-permute-start.23 = (bf16[4,2,256,512]{3,2,0,1:T(8,128)(2,1)S(1)}, bf16[4,2,256,512]{3,2,0,1:T(8,128)(2,1)S(1)}, u32[]{:S(2)}, u32[]{:S(2)}) collective-permute-start(bf16[4,2,256,512]{3,2,0,1:T(8,128)(2,1)S(1)} %pad_maximum_fusion.18), channel_id=1, source_target_pairs={{0,2},{1,3},{2,0},{3,1},{4,6},{5,7},{6,4},{7,5},{8,10},{9,11},{10,... | collective-permute-start | bytes 6291464 | tf_op jit(solution)/shard_map/ppermute | solution.py:29
  119.3 52.1 %collective-permute-start.4 = (bf16[1024,1536]{1,0:T(8,128)(2,1)S(1)}, bf16[1024,1536]{1,0:T(8,128)(2,1)}, u32[]{:S(2)}, u32[]{:S(2)}) collective-permute-start(bf16[1024,1536]{1,0:T(8,128)(2,1)S(1)} %bitcast.335), channel_id=1, source_target_pairs={{0,16},{16,0},{1,17},{17,1},{2,18},{18,2},{3,19},{19,3},{4,20},{20... | collective-permute-start | bytes 9437192 | tf_op jit(solution)/shard_map/ppermute | solution.py:34
  142.4 37.5 %collective-permute-start.19 = (bf16[1024,2048]{1,0:T(8,128)(2,1)}, bf16[1024,2048]{1,0:T(8,128)(2,1)}, u32[]{:S(2)}, u32[]{:S(2)}) collective-permute-start(bf16[1024,2048]{1,0:T(8,128)(2,1)} %bitcast.46), channel_id=1, source_target_pairs={{0,16},{16,0},{1,17},{17,1},{2,18},{18,2},{3,19},{19,3},{4,20},{20... | collective-permute-start | bytes 12582920 | tf_op jit(solution)/shard_map/ppermute | solution.py:34
  164.9 18.8 %collective-permute-start.24 = (bf16[4096,512]{1,0:T(8,128)(2,1)}, bf16[4096,512]{1,0:T(8,128)(2,1)}, u32[]{:S(2)}, u32[]{:S(2)}) collective-permute-start(bf16[4096,512]{1,0:T(8,128)(2,1)} %bitcast.57), channel_id=1, source_target_pairs={{0,16},{16,0},{1,17},{17,1},{2,18},{18,2},{3,19},{19,3},{4,20},{20... | collective-permute-start | bytes 12582920 | tf_op jit(solution)/shard_map/ppermute | solution.py:34
  314.4 16.6 %collective-permute-start.25 = (bf16[1,512,1024]{2,1,0:T(8,128)(2,1)}, bf16[1,512,1024]{2,1,0:T(8,128)(2,1)}, u32[]{:S(2)}, u32[]{:S(2)}) collective-permute-start(bf16[1,512,1024]{2,1,0:T(8,128)(2,1)} %slice.183), channel_id=1, source_target_pairs={{0,16},{16,0},{1,17},{17,1},{2,18},{18,2},{3,19},{19,3},{4,20},{20... | collective-permute-start | bytes 3145736 | tf_op jit(solution)/shard_map/ppermute | solution.py:34
  317.2 22.2 %collective-permute-start.38 = (bf16[1024,512]{1,0:T(8,128)(2,1)}, bf16[1024,512]{1,0:T(8,128)(2,1)}, u32[]{:S(2)}, u32[]{:S(2)}) collective-permute-start(bf16[1024,512]{1,0:T(8,128)(2,1)} %convolution_convert_fusion.4), channel_id=1, source_target_pairs={{0,16},{16,0},{1,17},{17,1},{2,18},{18,2},{3,19},{19,3},{4,20},{20... | collective-permute-start | bytes 3145736 | tf_op jit(solution)/shard_map/ppermute | solution.py:34
  324.1 59.5 %collective-permute-start.44 = (bf16[1024,2048]{1,0:T(8,128)(2,1)}, bf16[1024,2048]{1,0:T(8,128)(2,1)}, u32[]{:S(2)}, u32[]{:S(2)}) collective-permute-start(bf16[1024,2048]{1,0:T(8,128)(2,1)} %convolution_convert_fusion.1), channel_id=1, source_target_pairs={{0,16},{16,0},{1,17},{17,1},{2,18},{18,2},{3,19},{19,3},{4,20},{20... | collective-permute-start | bytes 12582920 | tf_op jit(solution)/shard_map/ppermute | solution.py:34
  329.2 74.6 %collective-permute-start.50 = (bf16[4096,512]{1,0:T(8,128)(2,1)}, bf16[4096,512]{1,0:T(8,128)(2,1)}, u32[]{:S(2)}, u32[]{:S(2)}) collective-permute-start(bf16[4096,512]{1,0:T(8,128)(2,1)} %convolution_convert_fusion), channel_id=1, source_target_pairs={{0,16},{16,0},{1,17},{17,1},{2,18},{18,2},{3,19},{19,3},{4,20},{20... | collective-permute-start | bytes 12582920 | tf_op jit(solution)/shard_map/ppermute | solution.py:34
  338.7 38.7 %collective-permute-start.27 = (bf16[1024,1536]{1,0:T(8,128)(2,1)}, bf16[1024,1536]{1,0:T(8,128)(2,1)}, u32[]{:S(2)}, u32[]{:S(2)}) collective-permute-start(bf16[1024,1536]{1,0:T(8,128)(2,1)} %fusion.13), channel_id=1, source_target_pairs={{0,16},{16,0},{1,17},{17,1},{2,18},{18,2},{3,19},{19,3},{4,20},{20... | collective-permute-start | bytes 9437192 | tf_op jit(solution)/shard_map/ppermute | solution.py:34
  382.0 20.5 %collective-permute-start.28 = (bf16[4,2,64,1536]{3,2,0,1:T(8,128)(2,1)S(1)}, bf16[4,2,64,1536]{3,2,0,1:T(8,128)(2,1)S(1)}, u32[]{:S(2)}, u32[]{:S(2)}) collective-permute-start(bf16[4,2,64,1536]{3,2,0,1:T(8,128)(2,1)S(1)} %pad_maximum_fusion.22), channel_id=1, source_target_pairs={{0,2},{1,3},{2,0},{3,1},{4,6},{5,7},{6,4},{7,5},{8,10},{9,11},{10,... | collective-permute-start | bytes 4718600 | tf_op jit(solution)/shard_map/ppermute | solution.py:29
  390.1 43.3 %collective-permute-start.45 = (bf16[4,2,64,2048]{3,2,0,1:T(8,128)(2,1)S(1)}, bf16[4,2,64,2048]{3,2,0,1:T(8,128)(2,1)S(1)}, u32[]{:S(2)}, u32[]{:S(2)}) collective-permute-start(bf16[4,2,64,2048]{3,2,0,1:T(8,128)(2,1)S(1)} %pad_maximum_fusion.19), channel_id=1, source_target_pairs={{0,2},{1,3},{2,0},{3,1},{4,6},{5,7},{6,4},{7,5},{8,10},{9,11},{10,... | collective-permute-start | bytes 6291464 | tf_op jit(solution)/shard_map/ppermute | solution.py:29
  403.2 20.5 %collective-permute-start.29 = (bf16[4,64,1536]{2,1,0:T(8,128)(2,1)S(1)}, bf16[4,64,1536]{2,1,0:T(8,128)(2,1)S(1)}, u32[]{:S(2)}, u32[]{:S(2)}) collective-permute-start(bf16[4,64,1536]{2,1,0:T(8,128)(2,1)S(1)} %dynamic-slice_bitcast_fusion.10), channel_id=1, source_target_pairs={{0,1},{1,0},{2,3},{3,2},{4,5},{5,4},{6,7},{7,6},{8,9},{9,8},{10,11... | collective-permute-start | bytes 2359304 | tf_op jit(solution)/shard_map/ppermute | solution.py:29
  410.3 56.8 %collective-permute-start.51 = (bf16[4,2,256,512]{3,2,0,1:T(8,128)(2,1)S(1)}, bf16[4,2,256,512]{3,2,0,1:T(8,128)(2,1)S(1)}, u32[]{:S(2)}, u32[]{:S(2)}) collective-permute-start(bf16[4,2,256,512]{3,2,0,1:T(8,128)(2,1)S(1)} %pad_maximum_fusion.20), channel_id=1, source_target_pairs={{0,2},{1,3},{2,0},{3,1},{4,6},{5,7},{6,4},{7,5},{8,10},{9,11},{10,... | collective-permute-start | bytes 6291464 | tf_op jit(solution)/shard_map/ppermute | solution.py:29
  434.3 34.2 %collective-permute-start.46 = (bf16[4,64,2048]{2,1,0:T(8,128)(2,1)S(1)}, bf16[4,64,2048]{2,1,0:T(8,128)(2,1)S(1)}, u32[]{:S(2)}, u32[]{:S(2)}) collective-permute-start(bf16[4,64,2048]{2,1,0:T(8,128)(2,1)S(1)} %dynamic-slice_bitcast_fusion.5), channel_id=1, source_target_pairs={{0,1},{1,0},{2,3},{3,2},{4,5},{5,4},{6,7},{7,6},{8,9},{9,8},{10,11... | collective-permute-start | bytes 3145736 | tf_op jit(solution)/shard_map/ppermute | solution.py:29
  435.0 33.3 %collective-permute-start.31 = (bf16[1,64,1536]{2,1,0:T(8,128)(2,1)S(1)}, bf16[1,64,1536]{2,1,0:T(8,128)(2,1)S(1)}, u32[]{:S(2)}, u32[]{:S(2)}) collective-permute-start(bf16[1,64,1536]{2,1,0:T(8,128)(2,1)S(1)} %constant_dynamic-slice_fusion.9), channel_id=1, source_target_pairs={{0,8},{1,9},{2,10},{3,11},{4,12},{5,13},{6,14},{7,15},{8,0},{9,1},... | collective-permute-start | bytes 589832 | tf_op jit(solution)/shard_map/ppermute | solution.py:29
  468.4 17.1 %collective-permute-start.32 = (bf16[64,1536]{1,0:T(8,128)(2,1)S(1)}, bf16[64,1536]{1,0:T(8,128)(2,1)S(1)}, u32[]{:S(2)}, u32[]{:S(2)}) collective-permute-start(bf16[64,1536]{1,0:T(8,128)(2,1)S(1)} %fusion.59), channel_id=1, source_target_pairs={{0,16},{16,0},{1,17},{17,1},{2,18},{18,2},{3,19},{19,3},{4,20},{20... | collective-permute-start | bytes 589832 | tf_op jit(solution)/shard_map/ppermute | solution.py:34
  469.0 16.6 %collective-permute-start.47 = (bf16[2,64,2048]{2,1,0:T(8,128)(2,1)S(1)}, bf16[2,64,2048]{2,1,0:T(8,128)(2,1)S(1)}, u32[]{:S(2)}, u32[]{:S(2)}) collective-permute-start(bf16[2,64,2048]{2,1,0:T(8,128)(2,1)S(1)} %dynamic-slice_bitcast_fusion.16), channel_id=1, source_target_pairs={{0,4},{1,5},{2,6},{3,7},{4,0},{5,1},{6,2},{7,3},{8,12},{9,13},{10,... | collective-permute-start | bytes 1572872 | tf_op jit(solution)/shard_map/ppermute | solution.py:29
  483.0 19.0 %collective-permute-start.53 = (bf16[2,256,512]{2,1,0:T(8,128)(2,1)S(1)}, bf16[2,256,512]{2,1,0:T(8,128)(2,1)S(1)}, u32[]{:S(2)}, u32[]{:S(2)}) collective-permute-start(bf16[2,256,512]{2,1,0:T(8,128)(2,1)S(1)} %dynamic-slice_bitcast_fusion.15), channel_id=1, source_target_pairs={{0,4},{1,5},{2,6},{3,7},{4,0},{5,1},{6,2},{7,3},{8,12},{9,13},{10,... | collective-permute-start | bytes 1572872 | tf_op jit(solution)/shard_map/ppermute | solution.py:29
  485.8 16.5 %collective-permute-start.48 = (bf16[1,64,2048]{2,1,0:T(8,128)(2,1)S(1)}, bf16[1,64,2048]{2,1,0:T(8,128)(2,1)S(1)}, u32[]{:S(2)}, u32[]{:S(2)}) collective-permute-start(bf16[1,64,2048]{2,1,0:T(8,128)(2,1)S(1)} %constant_dynamic-slice_fusion.1), channel_id=1, source_target_pairs={{0,8},{1,9},{2,10},{3,11},{4,12},{5,13},{6,14},{7,15},{8,0},{9,1},... | collective-permute-start | bytes 786440 | tf_op jit(solution)/shard_map/ppermute | solution.py:29
  (65 other events, 779.4 us)

commit v2 on v1

--- a/solution.py
+++ b/solution.py
@@ -61,7 +61,11 @@
     return part
 
 
-def gather_weight(shard):
+def after(array, earlier):
+    return lax.optimization_barrier((array, earlier))[0]
+
+
+def gather_weight(shard, earlier=None):
     own, even, along_x, along_y = places()
     width = shard.shape[1] // lax.axis_size("seq")
     held = lax.dynamic_slice_in_dim(shard, lax.axis_index("seq") * width, width, 1)[None]
@@ -75,6 +79,8 @@
     other = fsdp_swap(held, (1, 2))
     first = jnp.where(even, along_x, along_y) == 0
     held = jnp.stack([jnp.where(first, held, other), jnp.where(first, other, held)], axis=1)
+    if earlier is not None:
+        held = after(held, earlier)
     other = fsdp_swap(held, (2, 1))
     first = jnp.where(even, along_y, along_x) == 0
     near, far = jnp.where(first, held, other), jnp.where(first, other, held)
@@ -98,7 +104,7 @@
     return lax.dynamic_index_in_dim(array, index, axis, keepdims=False)
 
 
-def scatter_product(left, right):
+def scatter_parts(left, right):
     own, even, along_x, along_y = places()
     mine, bit = lax.axis_index("seq"), lax.axis_size("seq") // 2
     half = right.shape[1] // 2
@@ -110,7 +116,7 @@
             left, columns, (((0,), (0,)), ((), ())), preferred_element_type=F32
         )
 
-    arrived = seq_swap(product((1 - upper) * half).astype(LOW), bit)
+    arrived = seq_swap((yield product((1 - upper) * half).astype(LOW)), bit)
     total = product(upper * half) + arrived.astype(F32)
     while bit > 1:
         bit //= 2
@@ -124,10 +130,9 @@
     total = total.astype(LOW).reshape(span // 4, 4, rows, half)
     keep = [jnp.where(even, along_y * 2 + k, k * 2 + along_x) for k in (0, 1)]
     send = [jnp.where(even, (1 - along_y) * 2 + k, k * 2 + 1 - along_x) for k in (0, 1)]
+    leaving = yield jnp.stack([pick(total, place, 1) for place in send], axis=1)
     total = add_swapped(
-        jnp.stack([pick(total, place, 1) for place in keep], axis=1),
-        jnp.stack([pick(total, place, 1) for place in send], axis=1),
-        (2, 1),
+        jnp.stack([pick(total, place, 1) for place in keep], axis=1), leaving, (2, 1)
     ).astype(LOW)
     here = jnp.where(even, along_x, along_y)
     total = add_swapped(pick(total, here, 1), pick(total, 1 - here, 1), (1, 2))
@@ -135,7 +140,7 @@
         total = total.astype(LOW).reshape(-1, 2, rows, half)
         here = own // bit % 2
         total = add_swapped(pick(total, here, 1), pick(total, 1 - here, 1), (bit, bit))
-    return gather_seq(total.reshape(rows, half).astype(LOW)).astype(F32)
+    yield gather_seq(total.reshape(rows, half).astype(LOW)).astype(F32)
 
 
 def gather_vectors(vectors):
@@ -286,12 +291,11 @@
         ]
     )
     proj_all = gather_weight(proj_weight)
-    inner_all = gather_weight(inner_weight)
-    outer_all = gather_weight(outer_weight)
     gain_one, shift_one = gain_one.astype(F32), shift_one.astype(F32)
     gain_two, shift_two = gain_two.astype(F32), shift_two.astype(F32)
     joined_shift = jnp.concatenate([query_shift, jnp.zeros_like(query_shift), value_shift])
     joined = (jnp.dot(inputs, mix_all, preferred_element_type=F32) + joined_shift).astype(LOW)
+    inner_all = gather_weight(inner_weight, joined)
     queries = joined[:, :width].reshape(seq_count, token_rows, width)
     own_pairs = joined[:, width:].reshape(seq_count, token_rows, 2 * width)
     pairs = jnp.concatenate(
@@ -300,6 +304,7 @@
     length = token_rows * members
     rows_f32 = jax.ShapeDtypeStruct((seq_count, token_rows, width), F32)
     context, log_total = attention_call(attend_kernel, 2, [queries], pairs, [rows_f32, rows_f32])
+    outer_all = gather_weight(outer_weight, context)
     context_low = context.astype(LOW).reshape(all_rows, width)
     attended = jnp.dot(context_low, proj_all, preferred_element_type=F32) + proj_shift
     normed_one, first_pull = jax.vjp(
@@ -315,19 +320,29 @@
     grad_two, grad_gain_two, grad_shift_two = second_pull(upstream)
     grad_two_low = grad_two.astype(LOW)
     grad_outer_shift = jnp.sum(grad_two_low.astype(F32), axis=0)
-    grad_outer = scatter_product(active_low, grad_two_low)
+    outer_parts = scatter_parts(active_low, grad_two_low)
+    outer_sent, grad_two_low = lax.optimization_barrier((next(outer_parts), grad_two_low))
     grad_active = lax.dot_general(
         grad_two_low, outer_all, (((1,), (1,)), ((), ())), preferred_element_type=F32
     )
     (grad_inner_pre,) = gelu_pull(grad_active)
     inner_low = grad_inner_pre.astype(LOW)
     grad_inner_shift = jnp.sum(inner_low.astype(F32), axis=0)
-    grad_inner = scatter_product(normed_low, inner_low)
+    inner_parts = scatter_parts(normed_low, inner_low)
+    outer_sent, inner_sent, inner_low = lax.optimization_barrier(
+        (outer_parts.send(outer_sent), next(inner_parts), inner_low)
+    )
     grad_first = grad_two + jnp.dot(inner_low, inner_all.T, preferred_element_type=F32)
     grad_one, grad_gain_one, grad_shift_one = first_pull(grad_first)
     grad_one_low = grad_one.astype(LOW)
     grad_proj_shift = jnp.sum(grad_one_low.astype(F32), axis=0)
-    grad_proj = scatter_product(context_low, grad_one_low)
+    proj_parts = scatter_parts(context_low, grad_one_low)
+    inner_sent, proj_sent, grad_one_low = lax.optimization_barrier(
+        (inner_parts.send(inner_sent), next(proj_parts), grad_one_low)
+    )
+    grad_outer = outer_parts.send(outer_sent)
+    grad_inner = inner_parts.send(inner_sent)
+    grad_proj = proj_parts.send(proj_parts.send(proj_sent))
     grad_context = jnp.dot(grad_one_low, proj_all.T, preferred_element_type=F32).astype(LOW)
     pair_out = jax.ShapeDtypeStruct((seq_count, length, width), LOW)
     query_low, key_sums, value_sums = attention_call(
@@ -348,7 +363,8 @@
 
     key_low, value_low = to_owner(key_sums), to_owner(value_sums)
     joined_grad = jnp.concatenate([query_low, key_low, value_low], axis=1)
-    grad_mix = scatter_product(inputs, joined_grad)
+    mix_parts = scatter_parts(inputs, joined_grad)
+    grad_mix = mix_parts.send(mix_parts.send(next(mix_parts)))
     grad_query_shift = jnp.sum(query_low.astype(F32), axis=0)
     grad_value_shift = jnp.sum(value_low.astype(F32), axis=0)
     input_grad = (

time: 523 us -> 500 us (0.956)
  waiting for transfers between devices: 219 us -> 202 us
  other arithmetic: 45.2 us -> 57.7 us
  starting transfers between devices: 63.2 us -> 52.2 us
  matrix products: 104 us -> 98.4 us
    ppermute x40, waiting for transfers between devices: 216 us -> 201 us  [fsdp_swap(): return lax.ppermute(array, ('seq', 'fsdp'), pairs)]
    another operation x20, other arithmetic: 2.08 us -> 12.2 us  [gather_weight(): jnp.stack([jnp.where(first, held, other), jnp.where(first, other, held)],...]
    select_n x8, other arithmetic: 17.9 us -> 9.75 us  [gather_seq(): jnp.where(first, part, other)]
    ppermute x40, starting transfers between devices: 52.2 us -> 45.1 us  [fsdp_swap(): return lax.ppermute(array, ('seq', 'fsdp'), pairs)]
    unnamed x87 -> x105, local copies, waits for them, and re-layouts: 9.65 us -> 12.2 us
  transfers between devices with their start and end apart: 56 -> 56, of which waited for: 25 -> 26; matrix products, arithmetic and copies ran while one was open for 19% -> 31% of each run, Pallas kernels for 0% -> 10%
where the time goes in v2:
time: 500 us; the launch traced here: 496 us
  waiting for transfers between devices  202 us (40%)
  matrix products  98.4 us (20%)
  other arithmetic  57.7 us (12%)
  starting transfers between devices  52.2 us (10%)
  Pallas kernels  52 us (10%)
  local copies, waits for them, and re-layouts  32.2 us (6%)
    ppermute x40, waiting for transfers between devices, fsdp_swap(): return lax.ppermute(array, ('seq', 'fsdp'), pairs)  201 us
    pallas_call x2, Pallas kernels, attention_call(): pl.pallas_call(kernel, grid=(seqs, steps), in_specs=in_specs, out_specs=[...  52 us
    ppermute x40, starting transfers between devices, fsdp_swap(): return lax.ppermute(array, ('seq', 'fsdp'), pairs)  45.1 us
    dot_general x8, matrix products, product(): lax.dot_general(left, columns, (((0,), (0,)), ((), ())), preferred_elemen...  32.3 us
    dot_general x1, matrix products, on_device(): jnp.dot(normed_low, inner_all, preferred_element_type=F32) + inner_shift  26.5 us
    dot_general x1, matrix products, on_device(): lax.dot_general(grad_two_low, outer_all, (((1,), (1,)), ((), ())), prefer...  13.5 us
    another operation x20, other arithmetic, gather_weight(): jnp.stack([jnp.where(first, held, other), jnp.where(first, other, held)],...  12.2 us
    unnamed x105, local copies, waits for them, and re-layouts  12.2 us
  transfers between devices with their start and end apart: 56, of which 26 were waited for; matrix products, arithmetic and copies ran while one was open for 31% of the time, Pallas kernels for 10%

profile of v2, /device:TPU:0, one launch (start us, length us, event | category | flops | bytes accessed | tf_op | source)
XLA Modules:
  0.0 496.4 jit_solution(17639604103146056538)
XLA Ops:
  1.6 4.1 collective-permute-start
  5.7 9.1 %collective-permute-done = bf16[1,64,1536]{2,1,0:T(8,128)(2,1)S(1)} collective-permute-done((bf16[1,64,1536]{2,1,0:T(8,128)(2,1)S(1)}, bf16[1,64,1536]{2,1,0:T(8,128)(2,1)S(1)}, u32[]{:S(2)}, u32[]{:S(2)}) %collective-permute-start) | collective-permute-done | bytes 196640 | tf_op jit(solution)/shard_map/ppermute | solution.py:29
  16.7 6.1 %concatenate.48 = bf16[768]{0:T(1024)(128)(2,1)S(1)} concatenate(bf16[64]{0:T(256)(128)(2,1)} %param.17, bf16[64]{0:T(256)(128)(2,1)} %param.18, bf16[64]{0:T(256)(128)(2,1)} %param.20, bf16[64]{0:T(256)(128)(2,1)} %param.21, bf16[64]{0:T(256)(128)(2,1)} %param.22, bf16[256]{0:T(256)(128)(2,1)} %param.24, bf16[64]{0:T(256)(128)(2,1)} %param.26, bf16[64]{0:T(256)(128)(2,1)} %param.27, ...), dimensions={0} | concatenate | bytes 3072 | tf_op jit(solution)/shard_map/concatenate | solution.py:148
  37.3 4.5 collective-permute-done.2
  55.2 7.5 %collective-permute-done.3 = bf16[4,2,64,1536]{3,2,0,1:T(8,128)(2,1)} collective-permute-done((bf16[4,2,64,1536]{3,2,0,1:T(8,128)(2,1)S(1)}, bf16[4,2,64,1536]{3,2,0,1:T(8,128)(2,1)}, u32[]{:S(2)}, u32[]{:S(2)}) %collective-permute-start.3) | collective-permute-done | bytes 1572896 | tf_op jit(solution)/shard_map/ppermute | solution.py:29
  77.0 8.8 %collective-permute-done.21 = bf16[2,256,512]{2,1,0:T(8,128)(2,1)} collective-permute-done((bf16[2,256,512]{2,1,0:T(8,128)(2,1)}, bf16[2,256,512]{2,1,0:T(8,128)(2,1)}, u32[]{:S(2)}, u32[]{:S(2)}) %collective-permute-start.21) | collective-permute-done | bytes 524320 | tf_op jit(solution)/shard_map/ppermute | solution.py:29
  87.0 5.1 %collective-permute-done.17 = bf16[4,64,2048]{2,1,0:T(8,128)(2,1)} collective-permute-done((bf16[4,64,2048]{2,1,0:T(8,128)(2,1)}, bf16[4,64,2048]{2,1,0:T(8,128)(2,1)}, u32[]{:S(2)}, u32[]{:S(2)}) %collective-permute-start.17) | collective-permute-done | bytes 1048608 | tf_op jit(solution)/shard_map/ppermute | solution.py:29
  96.4 3.8 fusion.11
  104.7 23.2 %collective-permute-done.22 = bf16[4,256,512]{2,1,0:T(8,128)(2,1)S(1)} collective-permute-done((bf16[4,256,512]{2,1,0:T(8,128)(2,1)S(1)}, bf16[4,256,512]{2,1,0:T(8,128)(2,1)S(1)}, u32[]{:S(2)}, u32[]{:S(2)}) %collective-permute-start.22) | collective-permute-done | bytes 1048608 | tf_op jit(solution)/shard_map/ppermute | solution.py:29
  129.7 7.9 %collective-permute-done.18 = bf16[4,2,64,2048]{3,2,0,1:T(8,128)(2,1)S(1)} collective-permute-done((bf16[4,2,64,2048]{3,2,0,1:T(8,128)(2,1)S(1)}, bf16[4,2,64,2048]{3,2,0,1:T(8,128)(2,1)S(1)}, u32[]{:S(2)}, u32[]{:S(2)}) %collective-permute-start.18) | collective-permute-done | bytes 2097184 | tf_op jit(solution)/shard_map/ppermute | solution.py:29
  142.8 20.6 %shard_map.262 = (f32[1,512,1024]{2,1,0:T(8,128)S(1)}, f32[1,512,1024]{2,1,0:T(8,128)S(1)}) custom-call(bf16[1,512,1024]{2,1,0:T(8,128)(2,1)S(1)} %slice_bitcast_fusion.1.query_ref, bf16[1,1024,2048]{2,1,0:T(8,128)(2,1)S(1)} %pad_maximum_fusion.7.key_ref.value_ref, bf16[1,1024,2048]{2,1,0:T(8,128)(2,1)S(1)} %pad_maximum_fusion.7.key_ref.value_ref), custom_call_target="tpu_custom_call" | custom-call | flops 8589934592 | bytes 12582912 | tf_op jit(solution)/shard_map/pallas_call | solution.py:233
  169.0 22.1 %collective-permute-done.23 = bf16[4,2,256,512]{3,2,0,1:T(8,128)(2,1)} collective-permute-done((bf16[4,2,256,512]{3,2,0,1:T(8,128)(2,1)}, bf16[4,2,256,512]{3,2,0,1:T(8,128)(2,1)}, u32[]{:S(2)}, u32[]{:S(2)}) %collective-permute-start.23) | collective-permute-done | bytes 2097184 | tf_op jit(solution)/shard_map/ppermute | solution.py:29
  198.8 26.5 %multiply_convert_fusion = (bf16[512,4096]{1,0:T(8,128)(2,1)S(1)}, f32[512,4096]{1,0:T(8,128)}, f32[512,4096]{1,0:T(8,128)}) fusion(f32[4096]{0:T(1024)S(1)} %bitcast.352, bf16[1024,2048]{1,0:T(8,128)(2,1)S(1)} %get-tuple-element.65, bf16[1024,2048]{1,0:T(8,128)(2,1)S(1)} %get-tuple-element.64, f32[512,1024]{1,0:T(8,128)S(1)} %get-tuple-element.168, ...), kind=kOutput, calls=%fused_computation.8 | convolution fusion | flops 4452777984 | bytes 31485952 | tf_op jit(solution)/shard_map/dot_general | solution.py:314
  226.4 4.7 fusion.98
  234.4 4.4 convolution_convert_fusion
  239.4 13.5 %convert_reduce_fusion = (f32[4096]{0:T(1024)S(1)}, bf16[512,4096]{1,0:T(8,128)(2,1)}) fusion(f32[512,4096]{1,0:T(8,128)} %get-tuple-element.61, bf16[512,1024]{1,0:T(8,128)(2,1)S(1)} %get-tuple-element.34, bf16[4096,512]{1,0:T(8,128)(2,1)} %copy-done.21, bf16[4096,512]{1,0:T(8,128)(2,1)} %copy-done.20, f32[512,4096]{1,0:T(8,128)} %get-tuple-element.169, ...), kind=kOutput, calls=%fused_computation.4 | convolution fusion | flops 4347392000 | bytes 30441472 | tf_op jit(solution)/shard_map/dot_general | solution.py:325
  252.9 6.4 %convolution_convert_fusion.2 = bf16[1024,2048]{1,0:T(8,128)(2,1)} fusion(bf16[512,4096]{1,0:T(8,128)(2,1)} %get-tuple-element.35, s32[]{:T(128)S(6)} %select_n.837, f32[512,1024]{1,0:T(8,128)S(1)} %copy-done.13, f32[1024]{0:T(1024)S(1)} %reshape.428, f32[1024]{0:T(1024)S(1)} %reshape.427, f32[512]{0:T(512)S(1)} %fusion.80, f32[512]{0:T(512)S(1)} %broadcast_multiply_fusion.1), kind=kOutput, calls=%fused_computation.43 | convolution fusion | flops 2152202240 | bytes 8400900 | tf_op jit(solution)/shard_map/dot_general | solution.py:115
  259.3 4.7 add_convert_fusion.2
  267.5 25.9 %collective-permute-done.51 = bf16[4,2,256,512]{3,2,0,1:T(8,128)(2,1)} collective-permute-done((bf16[4,2,256,512]{3,2,0,1:T(8,128)(2,1)}, bf16[4,2,256,512]{3,2,0,1:T(8,128)(2,1)}, u32[]{:S(2)}, u32[]{:S(2)}) %collective-permute-start.51) | collective-permute-done | bytes 2097184 | tf_op jit(solution)/shard_map/ppermute | solution.py:29
  297.1 8.6 %multiply_reduce_fusion = (f32[1024]{0:T(1024)S(1)}, f32[512]{0:T(512)S(1)}, f32[1024]{0:T(1024)S(1)}, f32[512,1024]{1,0:T(8,128)S(1)}) fusion(f32[512,1024]{1,0:T(8,128)S(1)} %copy-done.14, f32[512]{0:T(512)S(1)} %fusion.80, f32[512]{0:T(512)S(1)} %broadcast_multiply_fusion.1, f32[1024]{0:T(1024)S(1)} %reshape.427, ...), kind=kOutput, calls=%fused_computation.72 | convolution fusion | flops 4316984832 | bytes 18894848 | tf_op jit(solution)/shard_map/dot_general | solution.py:335
  306.5 4.4 collective-permute-done.52
  313.9 9.6 %collective-permute-done.53 = bf16[2,256,512]{2,1,0:T(8,128)(2,1)S(1)} collective-permute-done((bf16[2,256,512]{2,1,0:T(8,128)(2,1)S(1)}, bf16[2,256,512]{2,1,0:T(8,128)(2,1)S(1)}, u32[]{:S(2)}, u32[]{:S(2)}) %collective-permute-start.53) | collective-permute-done | bytes 524320 | tf_op jit(solution)/shard_map/ppermute | solution.py:29
  324.8 4.8 add_convert_fusion
  335.6 31.4 %shard_map.263 = (bf16[1,512,1024]{2,1,0:T(8,128)(2,1)S(1)}, bf16[1,1024,1024]{2,1,0:T(8,128)(2,1)S(1)}, bf16[1,1024,1024]{2,1,0:T(8,128)(2,1)S(1)}) custom-call(bf16[1,512,1024]{2,1,0:T(8,128)(2,1)S(1)} %copy-done.7, bf16[1,1024,2048]{2,1,0:T(8,128)(2,1)} %copy-done.2, bf16[1,1024,2048]{2,1,0:T(8,128)(2,1)} %copy-done.2, ...), custom_call_target="tpu_custom_call" | custom-call | flops 21474836480 | bytes 12582912 | tf_op jit(solution)/shard_map/pallas_call | solution.py:233
  396.9 6.3 %fusion.32 = bf16[1,512,1024]{2,1,0:T(8,128)(2,1)} fusion(bf16[1024,1536]{1,0:T(8,128)(2,1)} %copy-done.33, bf16[1024,1536]{1,0:T(8,128)(2,1)S(1)} %copy-done.32, f32[512,1024]{1,0:T(8,128)S(1)} %copy-done.16, f32[512]{0:T(512)S(1)} %negate_multiply_fusion.1, bf16[512,1024]{1,0:T(8,128)(2,1)S(1)} %copy-done.28, bf16[512,1024]{1,0:T(8,128)(2,1)S(1)} %copy-done.26, ...), kind=kOutput, calls=%fused_computation.108 | convolution fusion | flops 3244818432 | bytes 12584960 | tf_op jit(solution)/shard_map/dot_general | solution.py:371
  403.7 4.4 collective-permute-done.41
  410.6 5.2 %collective-permute-done.42 = bf16[4,64,512]{2,1,0:T(8,128)(2,1)S(1)} collective-permute-done((bf16[4,64,512]{2,1,0:T(8,128)(2,1)S(1)}, bf16[4,64,512]{2,1,0:T(8,128)(2,1)S(1)}, u32[]{:S(2)}, u32[]{:S(2)}) %collective-permute-start.42) | collective-permute-done | bytes 262176 | tf_op jit(solution)/shard_map/ppermute | solution.py:29
  432.3 18.9 %collective-permute-done.47 = bf16[4,64,2048]{2,1,0:T(8,128)(2,1)S(1)} collective-permute-done((bf16[4,64,2048]{2,1,0:T(8,128)(2,1)S(1)}, bf16[4,64,2048]{2,1,0:T(8,128)(2,1)S(1)}, u32[]{:S(2)}, u32[]{:S(2)}) %collective-permute-start.47) | collective-permute-done | bytes 1048608 | tf_op jit(solution)/shard_map/ppermute | solution.py:29
  455.0 6.0 %collective-permute-done.48 = bf16[2,64,2048]{2,1,0:T(8,128)(2,1)S(1)} collective-permute-done((bf16[2,64,2048]{2,1,0:T(8,128)(2,1)S(1)}, bf16[2,64,2048]{2,1,0:T(8,128)(2,1)S(1)}, u32[]{:S(2)}, u32[]{:S(2)}) %collective-permute-start.48) | collective-permute-done | bytes 524320 | tf_op jit(solution)/shard_map/ppermute | solution.py:29
  466.7 7.0 %collective-permute-done.49 = bf16[1,64,2048]{2,1,0:T(8,128)(2,1)S(1)} collective-permute-done((bf16[1,64,2048]{2,1,0:T(8,128)(2,1)S(1)}, bf16[1,64,2048]{2,1,0:T(8,128)(2,1)S(1)}, u32[]{:S(2)}, u32[]{:S(2)}) %collective-permute-start.49) | collective-permute-done | bytes 262176 | tf_op jit(solution)/shard_map/ppermute | solution.py:29
  473.9 8.1 %collective-permute-done.32 = bf16[2,64,1536]{2,1,0:T(8,128)(2,1)S(1)} collective-permute-done((bf16[2,64,1536]{2,1,0:T(8,128)(2,1)S(1)}, bf16[2,64,1536]{2,1,0:T(8,128)(2,1)S(1)}, u32[]{:S(2)}, u32[]{:S(2)}) %collective-permute-start.32) | collective-permute-done | bytes 393248 | tf_op jit(solution)/shard_map/ppermute | solution.py:29
  482.4 11.3 %collective-permute-done.33 = bf16[1,64,1536]{2,1,0:T(8,128)(2,1)S(1)} collective-permute-done((bf16[1,64,1536]{2,1,0:T(8,128)(2,1)S(1)}, bf16[1,64,1536]{2,1,0:T(8,128)(2,1)S(1)}, u32[]{:S(2)}, u32[]{:S(2)}) %collective-permute-start.33) | collective-permute-done | bytes 196640 | tf_op jit(solution)/shard_map/ppermute | solution.py:29
  (367 shorter events, 159.4 us)
Async XLA Ops:
  1.6 13.2 %collective-permute-start = (bf16[1,64,1536]{2,1,0:T(8,128)(2,1)S(1)}, bf16[1,64,1536]{2,1,0:T(8,128)(2,1)S(1)}, u32[]{:S(2)}, u32[]{:S(2)}) collective-permute-start(bf16[1,64,1536]{2,1,0:T(8,128)(2,1)S(1)} %dynamic-slice_bitcast_fusion.25), channel_id=1, source_target_pairs={{0,8},{1,9},{2,10},{3,11},{4,12},{5,13},{6,14},{7,15},{8,0},{9,1},... | collective-permute-start | bytes 589832 | tf_op jit(solution)/shard_map/ppermute | solution.py:29
  15.9 13.6 %collective-permute-start.1 = (bf16[2,64,1536]{2,1,0:T(8,128)(2,1)S(1)}, bf16[2,64,1536]{2,1,0:T(8,128)(2,1)S(1)}, u32[]{:S(2)}, u32[]{:S(2)}) collective-permute-start(bf16[2,64,1536]{2,1,0:T(8,128)(2,1)S(1)} %maximum_bitcast_fusion.2), channel_id=1, source_target_pairs={{0,4},{1,5},{2,6},{3,7},{4,0},{5,1},{6,2},{7,3},{8,12},{9,13},{10,... | collective-permute-start | bytes 1179656 | tf_op jit(solution)/shard_map/ppermute | solution.py:29
  32.0 20.0 %collective-permute-start.15 = (bf16[1,64,2048]{2,1,0:T(8,128)(2,1)}, bf16[1,64,2048]{2,1,0:T(8,128)(2,1)S(1)}, u32[]{:S(2)}, u32[]{:S(2)}) collective-permute-start(bf16[1,64,2048]{2,1,0:T(8,128)(2,1)} %dynamic-slice_bitcast_fusion.24), channel_id=1, source_target_pairs={{0,8},{1,9},{2,10},{3,11},{4,12},{5,13},{6,14},{7,15},{8,0},{9,1},... | collective-permute-start | bytes 786440 | tf_op jit(solution)/shard_map/ppermute | solution.py:29
  35.7 15.4 %collective-permute-start.10 = (bf16[1,64,512]{2,1,0:T(8,128)(2,1)}, bf16[1,64,512]{2,1,0:T(8,128)(2,1)S(1)}, u32[]{:S(2)}, u32[]{:S(2)}) collective-permute-start(bf16[1,64,512]{2,1,0:T(8,128)(2,1)} %dynamic-slice_bitcast_fusion.27), channel_id=1, source_target_pairs={{0,8},{1,9},{2,10},{3,11},{4,12},{5,13},{6,14},{7,15},{8,0},{9,1},... | collective-permute-start | bytes 196616 | tf_op jit(solution)/shard_map/ppermute | solution.py:29
  42.0 20.6 %collective-permute-start.3 = (bf16[4,2,64,1536]{3,2,0,1:T(8,128)(2,1)S(1)}, bf16[4,2,64,1536]{3,2,0,1:T(8,128)(2,1)}, u32[]{:S(2)}, u32[]{:S(2)}) collective-permute-start(bf16[4,2,64,1536]{3,2,0,1:T(8,128)(2,1)S(1)} %pad_maximum_fusion.21), channel_id=1, source_target_pairs={{0,2},{1,3},{2,0},{3,1},{4,6},{5,7},{6,4},{7,5},{8,10},{9,11},{10,... | collective-permute-start | bytes 4718600 | tf_op jit(solution)/shard_map/ppermute | solution.py:29
  46.9 22.2 %collective-permute-start.20 = (bf16[1,256,512]{2,1,0:T(8,128)(2,1)}, bf16[1,256,512]{2,1,0:T(8,128)(2,1)}, u32[]{:S(2)}, u32[]{:S(2)}) collective-permute-start(bf16[1,256,512]{2,1,0:T(8,128)(2,1)} %dynamic-slice_bitcast_fusion.23), channel_id=1, source_target_pairs={{0,8},{1,9},{2,10},{3,11},{4,12},{5,13},{6,14},{7,15},{8,0},{9,1},... | collective-permute-start | bytes 786440 | tf_op jit(solution)/shard_map/ppermute | solution.py:29
  51.9 14.9 %collective-permute-start.11 = (bf16[2,64,512]{2,1,0:T(8,128)(2,1)S(1)}, bf16[2,64,512]{2,1,0:T(8,128)(2,1)S(1)}, u32[]{:S(2)}, u32[]{:S(2)}) collective-permute-start(bf16[2,64,512]{2,1,0:T(8,128)(2,1)S(1)} %maximum_bitcast_fusion.3), channel_id=1, source_target_pairs={{0,4},{1,5},{2,6},{3,7},{4,0},{5,1},{6,2},{7,3},{8,12},{9,13},{10,... | collective-permute-start | bytes 393224 | tf_op jit(solution)/shard_map/ppermute | solution.py:29
  53.1 17.0 %collective-permute-start.16 = (bf16[2,64,2048]{2,1,0:T(8,128)(2,1)S(1)}, bf16[2,64,2048]{2,1,0:T(8,128)(2,1)S(1)}, u32[]{:S(2)}, u32[]{:S(2)}) collective-permute-start(bf16[2,64,2048]{2,1,0:T(8,128)(2,1)S(1)} %maximum_bitcast_fusion), channel_id=1, source_target_pairs={{0,4},{1,5},{2,6},{3,7},{4,0},{5,1},{6,2},{7,3},{8,12},{9,13},{10,... | collective-permute-start | bytes 1572872 | tf_op jit(solution)/shard_map/ppermute | solution.py:29
  65.4 28.5 %collective-permute-start.4 = (bf16[1024,1536]{1,0:T(8,128)(2,1)S(1)}, bf16[1024,1536]{1,0:T(8,128)(2,1)}, u32[]{:S(2)}, u32[]{:S(2)}) collective-permute-start(bf16[1024,1536]{1,0:T(8,128)(2,1)S(1)} %bitcast.336), channel_id=1, source_target_pairs={{0,16},{16,0},{1,17},{17,1},{2,18},{18,2},{3,19},{19,3},{4,20},{20... | collective-permute-start | bytes 9437192 | tf_op jit(solution)/shard_map/ppermute | solution.py:34
  71.3 20.7 %collective-permute-start.17 = (bf16[4,64,2048]{2,1,0:T(8,128)(2,1)}, bf16[4,64,2048]{2,1,0:T(8,128)(2,1)}, u32[]{:S(2)}, u32[]{:S(2)}) collective-permute-start(bf16[4,64,2048]{2,1,0:T(8,128)(2,1)} %bitcast.43), channel_id=1, source_target_pairs={{0,1},{1,0},{2,3},{3,2},{4,5},{5,4},{6,7},{7,6},{8,9},{9,8},{10,11... | collective-permute-start | bytes 3145736 | tf_op jit(solution)/shard_map/ppermute | solution.py:29
  72.7 13.1 %collective-permute-start.21 = (bf16[2,256,512]{2,1,0:T(8,128)(2,1)}, bf16[2,256,512]{2,1,0:T(8,128)(2,1)}, u32[]{:S(2)}, u32[]{:S(2)}) collective-permute-start(bf16[2,256,512]{2,1,0:T(8,128)(2,1)} %maximum_bitcast_fusion.1), channel_id=1, source_target_pairs={{0,4},{1,5},{2,6},{3,7},{4,0},{5,1},{6,2},{7,3},{8,12},{9,13},{10,... | collective-permute-start | bytes 1572872 | tf_op jit(solution)/shard_map/ppermute | solution.py:29
  75.4 26.6 %collective-permute-start.13 = (bf16[4,2,64,512]{3,2,0,1:T(8,128)(2,1)S(1)}, bf16[4,2,64,512]{3,2,0,1:T(8,128)(2,1)S(1)}, u32[]{:S(2)}, u32[]{:S(2)}) collective-permute-start(bf16[4,2,64,512]{3,2,0,1:T(8,128)(2,1)S(1)} %pad_maximum_fusion.37), channel_id=1, source_target_pairs={{0,2},{1,3},{2,0},{3,1},{4,6},{5,7},{6,4},{7,5},{8,10},{9,11},{10,... | collective-permute-start | bytes 1572872 | tf_op jit(solution)/shard_map/ppermute | solution.py:29
  100.2 37.3 %collective-permute-start.18 = (bf16[4,2,64,2048]{3,2,0,1:T(8,128)(2,1)S(1)}, bf16[4,2,64,2048]{3,2,0,1:T(8,128)(2,1)S(1)}, u32[]{:S(2)}, u32[]{:S(2)}) collective-permute-start(bf16[4,2,64,2048]{3,2,0,1:T(8,128)(2,1)S(1)} %pad_maximum_fusion.17), channel_id=1, source_target_pairs={{0,2},{1,3},{2,0},{3,1},{4,6},{5,7},{6,4},{7,5},{8,10},{9,11},{10,... | collective-permute-start | bytes 6291464 | tf_op jit(solution)/shard_map/ppermute | solution.py:29
  101.9 26.0 %collective-permute-start.22 = (bf16[4,256,512]{2,1,0:T(8,128)(2,1)S(1)}, bf16[4,256,512]{2,1,0:T(8,128)(2,1)S(1)}, u32[]{:S(2)}, u32[]{:S(2)}) collective-permute-start(bf16[4,256,512]{2,1,0:T(8,128)(2,1)S(1)} %bitcast.341), channel_id=1, source_target_pairs={{0,1},{1,0},{2,3},{3,2},{4,5},{5,4},{6,7},{7,6},{8,9},{9,8},{10,11... | collective-permute-start | bytes 3145736 | tf_op jit(solution)/shard_map/ppermute | solution.py:29
  102.4 63.4 %collective-permute-start.14 = (bf16[1024,512]{1,0:T(8,128)(2,1)S(1)}, bf16[1024,512]{1,0:T(8,128)(2,1)}, u32[]{:S(2)}, u32[]{:S(2)}) collective-permute-start(bf16[1024,512]{1,0:T(8,128)(2,1)S(1)} %bitcast.340), channel_id=1, source_target_pairs={{0,16},{16,0},{1,17},{17,1},{2,18},{18,2},{3,19},{19,3},{4,20},{20... | collective-permute-start | bytes 3145736 | tf_op jit(solution)/shard_map/ppermute | solution.py:34
  104.6 37.5 %collective-permute-start.9 = (bf16[1,512,2048]{2,1,0:T(8,128)(2,1)S(1)}, bf16[1,512,2048]{2,1,0:T(8,128)(2,1)S(1)}, u32[]{:S(2)}, u32[]{:S(2)}) collective-permute-start(bf16[1,512,2048]{2,1,0:T(8,128)(2,1)S(1)} %slice_bitcast_fusion), channel_id=1, source_target_pairs={{0,16},{16,0},{1,17},{17,1},{2,18},{18,2},{3,19},{19,3},{4,20},{20... | collective-permute-start | bytes 6291464 | tf_op jit(solution)/shard_map/ppermute | solution.py:34
  141.0 54.0 %collective-permute-start.19 = (bf16[1024,2048]{1,0:T(8,128)(2,1)}, bf16[1024,2048]{1,0:T(8,128)(2,1)}, u32[]{:S(2)}, u32[]{:S(2)}) collective-permute-start(bf16[1024,2048]{1,0:T(8,128)(2,1)} %bitcast.46), channel_id=1, source_target_pairs={{0,16},{16,0},{1,17},{17,1},{2,18},{18,2},{3,19},{19,3},{4,20},{20... | collective-permute-start | bytes 12582920 | tf_op jit(solution)/shard_map/ppermute | solution.py:34
  164.8 26.4 %collective-permute-start.23 = (bf16[4,2,256,512]{3,2,0,1:T(8,128)(2,1)}, bf16[4,2,256,512]{3,2,0,1:T(8,128)(2,1)}, u32[]{:S(2)}, u32[]{:S(2)}) collective-permute-start(bf16[4,2,256,512]{3,2,0,1:T(8,128)(2,1)} %pad_maximum_fusion.18), channel_id=1, source_target_pairs={{0,2},{1,3},{2,0},{3,1},{4,6},{5,7},{6,4},{7,5},{8,10},{9,11},{10,... | collective-permute-start | bytes 6291464 | tf_op jit(solution)/shard_map/ppermute | solution.py:29
  194.9 30.4 %collective-permute-start.24 = (bf16[4096,512]{1,0:T(8,128)(2,1)S(1)}, bf16[4096,512]{1,0:T(8,128)(2,1)S(1)}, u32[]{:S(2)}, u32[]{:S(2)}) collective-permute-start(bf16[4096,512]{1,0:T(8,128)(2,1)S(1)} %bitcast.335), channel_id=1, source_target_pairs={{0,16},{16,0},{1,17},{17,1},{2,18},{18,2},{3,19},{19,3},{4,20},{20... | collective-permute-start | bytes 12582920 | tf_op jit(solution)/shard_map/ppermute | solution.py:34
  238.9 20.4 %collective-permute-start.25 = (bf16[4096,512]{1,0:T(8,128)(2,1)}, bf16[4096,512]{1,0:T(8,128)(2,1)}, u32[]{:S(2)}, u32[]{:S(2)}) collective-permute-start(bf16[4096,512]{1,0:T(8,128)(2,1)} %convolution_convert_fusion), channel_id=1, source_target_pairs={{0,16},{16,0},{1,17},{17,1},{2,18},{18,2},{3,19},{19,3},{4,20},{20... | collective-permute-start | bytes 12582920 | tf_op jit(solution)/shard_map/ppermute | solution.py:34
  267.0 26.4 %collective-permute-start.51 = (bf16[4,2,256,512]{3,2,0,1:T(8,128)(2,1)}, bf16[4,2,256,512]{3,2,0,1:T(8,128)(2,1)}, u32[]{:S(2)}, u32[]{:S(2)}) collective-permute-start(bf16[4,2,256,512]{3,2,0,1:T(8,128)(2,1)} %pad_maximum_fusion.19), channel_id=1, source_target_pairs={{0,2},{1,3},{2,0},{3,1},{4,6},{5,7},{6,4},{7,5},{8,10},{9,11},{10,... | collective-permute-start | bytes 6291464 | tf_op jit(solution)/shard_map/ppermute | solution.py:29
  267.5 57.4 %collective-permute-start.26 = (bf16[1024,2048]{1,0:T(8,128)(2,1)}, bf16[1024,2048]{1,0:T(8,128)(2,1)}, u32[]{:S(2)}, u32[]{:S(2)}) collective-permute-start(bf16[1024,2048]{1,0:T(8,128)(2,1)} %convolution_convert_fusion.2), channel_id=1, source_target_pairs={{0,16},{16,0},{1,17},{17,1},{2,18},{18,2},{3,19},{19,3},{4,20},{20... | collective-permute-start | bytes 12582920 | tf_op jit(solution)/shard_map/ppermute | solution.py:34
  296.0 14.9 %collective-permute-start.52 = (bf16[4,256,512]{2,1,0:T(8,128)(2,1)S(1)}, bf16[4,256,512]{2,1,0:T(8,128)(2,1)S(1)}, u32[]{:S(2)}, u32[]{:S(2)}) collective-permute-start(bf16[4,256,512]{2,1,0:T(8,128)(2,1)S(1)} %dynamic-slice_bitcast_fusion), channel_id=1, source_target_pairs={{0,1},{1,0},{2,3},{3,2},{4,5},{5,4},{6,7},{7,6},{8,9},{9,8},{10,11... | collective-permute-start | bytes 3145736 | tf_op jit(solution)/shard_map/ppermute | solution.py:29
  323.7 49.8 %collective-permute-start.54 = (bf16[1,256,512]{2,1,0:T(8,128)(2,1)S(1)}, bf16[1,256,512]{2,1,0:T(8,128)(2,1)}, u32[]{:S(2)}, u32[]{:S(2)}) collective-permute-start(bf16[1,256,512]{2,1,0:T(8,128)(2,1)S(1)} %constant_dynamic-slice_fusion), channel_id=1, source_target_pairs={{0,8},{1,9},{2,10},{3,11},{4,12},{5,13},{6,14},{7,15},{8,0},{9,1},... | collective-permute-start | bytes 786440 | tf_op jit(solution)/shard_map/ppermute | solution.py:29
  375.6 13.6 %collective-permute-start.40 = (bf16[1024,512]{1,0:T(8,128)(2,1)}, bf16[1024,512]{1,0:T(8,128)(2,1)}, u32[]{:S(2)}, u32[]{:S(2)}) collective-permute-start(bf16[1024,512]{1,0:T(8,128)(2,1)} %convolution_convert_fusion.4), channel_id=1, source_target_pairs={{0,16},{16,0},{1,17},{17,1},{2,18},{18,2},{3,19},{19,3},{4,20},{20... | collective-permute-start | bytes 3145736 | tf_op jit(solution)/shard_map/ppermute | solution.py:34
  376.1 46.8 %collective-permute-start.46 = (bf16[4,2,64,2048]{3,2,0,1:T(8,128)(2,1)}, bf16[4,2,64,2048]{3,2,0,1:T(8,128)(2,1)}, u32[]{:S(2)}, u32[]{:S(2)}) collective-permute-start(bf16[4,2,64,2048]{3,2,0,1:T(8,128)(2,1)} %pad_maximum_fusion.20), channel_id=1, source_target_pairs={{0,2},{1,3},{2,0},{3,1},{4,6},{5,7},{6,4},{7,5},{8,10},{9,11},{10,... | collective-permute-start | bytes 6291464 | tf_op jit(solution)/shard_map/ppermute | solution.py:29
  388.5 37.6 %collective-permute-start.29 = (bf16[1024,1536]{1,0:T(8,128)(2,1)}, bf16[1024,1536]{1,0:T(8,128)(2,1)}, u32[]{:S(2)}, u32[]{:S(2)}) collective-permute-start(bf16[1024,1536]{1,0:T(8,128)(2,1)} %fusion.13), channel_id=1, source_target_pairs={{0,16},{16,0},{1,17},{17,1},{2,18},{18,2},{3,19},{19,3},{4,20},{20... | collective-permute-start | bytes 9437192 | tf_op jit(solution)/shard_map/ppermute | solution.py:34
  393.2 14.9 %collective-permute-start.41 = (bf16[4,2,64,512]{3,2,0,1:T(8,128)(2,1)}, bf16[4,2,64,512]{3,2,0,1:T(8,128)(2,1)}, u32[]{:S(2)}, u32[]{:S(2)}) collective-permute-start(bf16[4,2,64,512]{3,2,0,1:T(8,128)(2,1)} %pad_maximum_fusion.38), channel_id=1, source_target_pairs={{0,2},{1,3},{2,0},{3,1},{4,6},{5,7},{6,4},{7,5},{8,10},{9,11},{10,... | collective-permute-start | bytes 1572872 | tf_op jit(solution)/shard_map/ppermute | solution.py:29
  417.7 13.2 %collective-permute-start.39 = (f32[1,768]{1,0:T(1,128)S(1)}, f32[1,768]{1,0:T(1,128)S(1)}, u32[]{:S(2)}, u32[]{:S(2)}) collective-permute-start(f32[1,768]{1,0:T(1,128)S(1)} %constant_dynamic-slice_fusion.3), channel_id=1, source_target_pairs={{0,1},{1,0},{2,3},{3,2},{4,5},{5,4},{6,7},{7,6},{8,9},{9,8},{10,11... | collective-permute-start | bytes 9224 | tf_op jit(solution)/shard_map/ppermute | solution.py:29
  425.6 25.6 %collective-permute-start.47 = (bf16[4,64,2048]{2,1,0:T(8,128)(2,1)S(1)}, bf16[4,64,2048]{2,1,0:T(8,128)(2,1)S(1)}, u32[]{:S(2)}, u32[]{:S(2)}) collective-permute-start(bf16[4,64,2048]{2,1,0:T(8,128)(2,1)S(1)} %dynamic-slice_bitcast_fusion.3), channel_id=1, source_target_pairs={{0,1},{1,0},{2,3},{3,2},{4,5},{5,4},{6,7},{7,6},{8,9},{9,8},{10,11... | collective-permute-start | bytes 3145736 | tf_op jit(solution)/shard_map/ppermute | solution.py:29
  430.3 23.1 %collective-permute-start.30 = (bf16[4,2,64,1536]{3,2,0,1:T(8,128)(2,1)S(1)}, bf16[4,2,64,1536]{3,2,0,1:T(8,128)(2,1)S(1)}, u32[]{:S(2)}, u32[]{:S(2)}) collective-permute-start(bf16[4,2,64,1536]{3,2,0,1:T(8,128)(2,1)S(1)} %pad_maximum_fusion.22), channel_id=1, source_target_pairs={{0,2},{1,3},{2,0},{3,1},{4,6},{5,7},{6,4},{7,5},{8,10},{9,11},{10,... | collective-permute-start | bytes 4718600 | tf_op jit(solution)/shard_map/ppermute | solution.py:29
  466.2 15.7 %collective-permute-start.32 = (bf16[2,64,1536]{2,1,0:T(8,128)(2,1)S(1)}, bf16[2,64,1536]{2,1,0:T(8,128)(2,1)S(1)}, u32[]{:S(2)}, u32[]{:S(2)}) collective-permute-start(bf16[2,64,1536]{2,1,0:T(8,128)(2,1)S(1)} %dynamic-slice_bitcast_fusion.17), channel_id=1, source_target_pairs={{0,4},{1,5},{2,6},{3,7},{4,0},{5,1},{6,2},{7,3},{8,12},{9,13},{10,... | collective-permute-start | bytes 1179656 | tf_op jit(solution)/shard_map/ppermute | solution.py:29
  (74 other events, 589.4 us)
